TPU v7x, 512 devices: a whole 4x4x16 slice. The times are simulated.
512 devices in a mesh: row: 32 (over y, z_hi, core), col: 16 (over x, z_lo).
Axes of the slice: x: 4, y: 4, z: 16 (z_hi: 4, z_lo: 4; z = z_hi * 4 + z_lo), core: 2. Of those that a mesh axis runs over, the one named last changes fastest.
Arguments:
- node_latents: bfloat16 [65536, 512], P(('row', 'col')), may hold values from -6 to 6
- fine_edges: bfloat16 [524288, 512], P(('row', 'col')), may hold values from -6 to 6
- fine_senders: int32 [524288], P(('row', 'col')), may hold values from 0 to 767, as said below
- degrees: int32 [65536], P(('row', 'col')), may hold values from 5 to 8, as said below
- send_list: int32 [65536], P(('row', 'col')), may hold values from 0 to 127
- coarse_row: int32 [512], P(('row', 'col')), may hold values from 0 to 127
- coarse_edges: bfloat16 [8192, 512], P(('row', 'col')), may hold values from -6 to 6
- coarse_senders: int32 [8192], P(('row', 'col')), may hold values from 0 to 511
- w_edge: bfloat16 [512, 512], replicated, may hold values from -0.15625 to 0.15625
- w_sender: bfloat16 [512, 512], replicated, may hold values from -0.15625 to 0.15625
- w_receiver: bfloat16 [512, 512], replicated, may hold values from -0.15625 to 0.15625
- w_message: bfloat16 [512, 512], replicated, may hold values from -0.25 to 0.25
- w_node: bfloat16 [512, 512], replicated, may hold values from -0.1875 to 0.1875
- w_gather: bfloat16 [512, 512], replicated, may hold values from -0.1875 to 0.1875
- w_node_out: bfloat16 [512, 512], replicated, may hold values from -0.25 to 0.25
Outputs:
- new_nodes: bfloat16 [65536, 512], P(('row', 'col'))
Inputs may be any that keep to these rules, and one draw needn't show every extreme that they name: `fine_senders`: rows below 128 are the partition's own nodes, the next 128 its received rows in direction order, the last 512 the coarse nodes. `degrees`: the first node of every partition uses all 8 slots.
All inputs are finite; a program needn't handle non-finite values.
Results may differ from a plain program's by a relative error of at most 0.0045.
The roundings to bfloat16 on the way count: a program that leaves them out, or rounds other values in their place, can miss the bound.
Values may be sent and summed in bfloat16 or wider, within the bound.
No kernel may reach another device: no remote copies, remote signals or barrier semaphores. Data moves between devices by JAX's collectives and lax.ppermute only.
A program may use at most 64 MiB of HBM per device.

v0:
```python
import jax
import jax.numpy as jnp
from jax import lax
from jax.sharding import PartitionSpec as P

epsilon = 1e-05
DIRECTIONS = ((-1, -1), (-1, 0), (-1, 1), (0, -1), (0, 1), (1, -1), (1, 0), (1, 1))


def with_halo(shard, sides, width):
    for axis, dim in sides:
        devices, length = (lax.axis_size(axis), shard.shape[dim])
        up = [(i, (i + 1) % devices) for i in range(devices)]
        down = [(j, i) for i, j in up]
        last = lax.slice_in_dim(shard, length - width, length, axis=dim)
        initial = lax.slice_in_dim(shard, 0, width, axis=dim)
        before = lax.ppermute(last, axis, up)
        after = lax.ppermute(initial, axis, down)
        shard = jnp.concatenate([before, shard, after], axis=dim)
    return shard


def layer_norm(values):
    centred = values - jnp.mean(values, axis=-1, keepdims=True)
    second = jnp.mean(centred * centred, axis=-1, keepdims=True)
    return centred * lax.rsqrt(second + epsilon)


def edge_update(latents, from_sender, from_receiver, w_edge, w_message):
    before = (
        jnp.dot(latents, w_edge, preferred_element_type=jnp.float32) + from_sender + from_receiver
    )
    hidden = jax.nn.silu(before).astype(jnp.bfloat16)
    message = layer_norm(jnp.dot(hidden, w_message, preferred_element_type=jnp.float32))
    return latents.astype(jnp.float32) + message


def body(
    node_latents,
    fine_edges,
    fine_senders,
    degrees,
    send_list,
    coarse_row,
    coarse_edges,
    coarse_senders,
    w_edge,
    w_sender,
    w_receiver,
    w_message,
    w_node,
    w_gather,
    w_node_out,
):
    node_count, latent = node_latents.shape
    per_node = fine_edges.shape[0] // node_count
    send_count = send_list.shape[0] // 8
    outgoing = jnp.take(node_latents, send_list, axis=0).reshape(8, send_count, latent)
    own_coarse = jnp.take(node_latents, coarse_row, axis=0)
    coarse_recv_own = jnp.dot(own_coarse, w_receiver, preferred_element_type=jnp.float32)
    coarse_send = jnp.dot(
        lax.all_gather(own_coarse, ("row", "col"), axis=0, tiled=True),
        w_sender,
        preferred_element_type=jnp.float32,
    )
    own_sender = jnp.dot(node_latents, w_sender, preferred_element_type=jnp.float32)
    receiver_proj = jnp.dot(node_latents, w_receiver, preferred_element_type=jnp.float32)
    centre = jnp.zeros((1, send_count, latent), jnp.bfloat16)
    layout = jnp.concatenate([outgoing[:4], centre, outgoing[4:]], axis=0).reshape(
        3, 3, send_count, latent
    )
    padded = with_halo(layout, (("row", 0), ("col", 1)), 1)
    received = jnp.stack([padded[2 + 2 * offsets[0], 2 + 2 * offsets[1]] for offsets in DIRECTIONS])
    received = received.reshape(8 * send_count, latent)
    halo_sender = jnp.dot(received, w_sender, preferred_element_type=jnp.float32)
    sender_proj = jnp.concatenate([own_sender, halo_sender, coarse_send], axis=0)
    coarse_updated = edge_update(
        coarse_edges,
        jnp.take(coarse_send, coarse_senders, axis=0),
        coarse_recv_own,
        w_edge,
        w_message,
    )
    own_share = jnp.sum(coarse_updated, axis=0, keepdims=True)
    updated = edge_update(
        fine_edges,
        jnp.take(sender_proj, fine_senders, axis=0),
        jnp.repeat(receiver_proj, per_node, axis=0),
        w_edge,
        w_message,
    )
    updated = updated.reshape(node_count, per_node, latent)
    in_use = lax.broadcasted_iota(jnp.int32, (node_count, per_node), 1) < degrees[:, None]
    aggregate = jnp.sum(jnp.where(in_use[:, :, None], updated, jnp.zeros_like(updated)), axis=1)
    at_owner = (lax.broadcasted_iota(jnp.int32, (node_count, 1), 0) == coarse_row[0]).astype(
        jnp.float32
    )
    summed = (aggregate + at_owner * own_share).astype(jnp.bfloat16)
    node_hidden = jax.nn.silu(
        jnp.dot(node_latents, w_node, preferred_element_type=jnp.float32)
        + jnp.dot(summed, w_gather, preferred_element_type=jnp.float32)
    ).astype(jnp.bfloat16)
    result = node_latents.astype(jnp.float32) + layer_norm(
        jnp.dot(node_hidden, w_node_out, preferred_element_type=jnp.float32)
    )
    return result.astype(jnp.bfloat16)


def solution(mesh):
    placed = (
        P(("row", "col"), None),
        P(("row", "col"), None),
        P(("row", "col")),
        P(("row", "col")),
        P(("row", "col")),
        P(("row", "col")),
        P(("row", "col"), None),
        P(("row", "col")),
        P(),
        P(),
        P(),
        P(),
        P(),
        P(),
        P(),
    )
    return jax.shard_map(
        body, mesh=mesh, in_specs=placed, out_specs=P(("row", "col"), None), check_vma=False
    )
```

profile of v0, /device:TPU:102, one launch (start us, length us, event | category | flops | bytes accessed | tf_op | source)
XLA Modules:
  0.0 1313.3 jit_solution(7765184659225842244)
XLA Ops:
  0.0 0.8 compare_and_fusion.2
  1.5 1.9 gather_fusion
  4.1 11.9 collective-permute-start.1
  16.0 1.9 collective-permute-start
  17.9 1.2 compare_and_fusion.1
  21.2 0.7 fusion.38
  21.9 1.8 fusion.31
  23.7 1.0 fusion.47
  26.5 0.9 fusion.44
  27.7 1217.5 %all-gather = bf16[512,1,512]{2,1,0:T(2,128)(2,1)S(1)} all-gather(bf16[1,1,512]{2,1,0:T(2,128)(2,1)S(1)} %fusion.38), channel_id=1, replica_groups=mesh['row'=32,'col'=16] {'row','col'}, dimensions={0}, use_global_device_ids=true | all-gather | bytes 525312 | tf_op jit(solution)/shard_map/all_gather | solution.py:62
  1246.3 1.5 fusion.42
  1248.1 1.0 pad_maximum_fusion.1
  1249.8 0.8 pad_maximum_fusion.2
  1250.6 37.8 %collective-permute-start.2 = (bf16[5,1,16,512]{3,2,1,0:T(8,128)(2,1)S(1)}, bf16[5,1,16,512]{3,2,1,0:T(8,128)(2,1)S(1)}, u32[]{:S(2)}, u32[]{:S(2)}) collective-permute-start(bf16[5,1,16,512]{3,2,1,0:T(8,128)(2,1)S(1)} %get-tuple-element.17), channel_id=1, source_target_pairs={{0,1},{1,2},{2,3},{3,4},{4,5},{5,6},{6,7},{7,8},{8,9},{9,10},{10,1... | collective-permute-start | bytes 245768 | tf_op jit(solution)/shard_map/ppermute | solution.py:17
  1288.4 1.9 collective-permute-start.3
  1290.4 0.7 fusion.24
  1291.1 7.5 collective-permute-done.3
  1298.6 0.7 fusion.19
  1299.8 4.9 gather_fusion.1
  1304.7 3.5 fusion.41
  1308.7 0.7 copy-done.4
  1309.4 1.0 fusion
  1310.5 1.8 fusion.43
  1312.5 0.8 add_convert_fusion
  (66 shorter events, 8.1 us)
Async XLA Ops:
  0.0 1246.3 %copy-start = (bf16[512,512]{1,0:T(8,128)(2,1)S(1)}, bf16[512,512]{1,0:T(8,128)(2,1)}, u32[]{:S(2)}) copy-start(bf16[512,512]{1,0:T(8,128)(2,1)} %param.26) | copy-start | bytes 1572868
  0.0 23.7 %copy-start.1 = (bf16[128,512]{1,0:T(8,128)(2,1)S(1)}, bf16[128,512]{1,0:T(8,128)(2,1)}, u32[]{:S(2)}) copy-start(bf16[128,512]{1,0:T(8,128)(2,1)} %param.15) | copy-start | bytes 393220
  0.0 23.7 %copy-start.3 = (bf16[512,512]{1,0:T(8,128)(2,1)S(1)}, bf16[512,512]{1,0:T(8,128)(2,1)}, u32[]{:S(2)}) copy-start(bf16[512,512]{1,0:T(8,128)(2,1)} %param.25) | copy-start | bytes 1572868
  0.0 24.6 %copy-start.12 = (s32[1024]{0:T(1024)S(1)}, s32[1024]{0:T(1024)}, u32[]{:S(2)}) copy-start(s32[1024]{0:T(1024)} %param.17) | copy-start | bytes 12292
  0.0 25.8 %copy-start.15 = (s32[128]{0:T(128)S(1)}, s32[128]{0:T(128)}, u32[]{:S(2)}) copy-start(s32[128]{0:T(128)} %param.18) | copy-start | bytes 1540
  0.0 26.5 %copy-start.5 = (bf16[512,512]{1,0:T(8,128)(2,1)S(1)}, bf16[512,512]{1,0:T(8,128)(2,1)}, u32[]{:S(2)}) copy-start(bf16[512,512]{1,0:T(8,128)(2,1)} %param.27) | copy-start | bytes 1572868
  1.5 26.0 %copy-start.2 = (bf16[512,512]{1,0:T(8,128)(2,1)S(1)}, bf16[512,512]{1,0:T(8,128)(2,1)}, u32[]{:S(2)}) copy-start(bf16[512,512]{1,0:T(8,128)(2,1)} %param.24) | copy-start | bytes 1572868
  4.1 1245.7 %collective-permute-start.1 = (bf16[1,3,16,512]{3,2,1,0:T(8,128)(2,1)}, bf16[1,3,16,512]{3,2,1,0:T(8,128)(2,1)}, u32[]{:S(2)}, u32[]{:S(2)}) collective-permute-start(bf16[1,3,16,512]{3,2,1,0:T(8,128)(2,1)} %bitcast.4), channel_id=1, source_target_pairs={{16,0},{32,16},{48,32},{64,48},{80,64},{96,80},{112,96},{128,112},... | collective-permute-start | bytes 147464 | tf_op jit(solution)/shard_map/ppermute | solution.py:18
  16.0 1233.8 %collective-permute-start = (bf16[1,3,16,512]{3,2,1,0:T(8,128)(2,1)}, bf16[1,3,16,512]{3,2,1,0:T(8,128)(2,1)}, u32[]{:S(2)}, u32[]{:S(2)}) collective-permute-start(bf16[1,3,16,512]{3,2,1,0:T(8,128)(2,1)} %bitcast), channel_id=1, source_target_pairs={{0,16},{16,32},{32,48},{48,64},{64,80},{80,96},{96,112},{112,128},... | collective-permute-start | bytes 147464 | tf_op jit(solution)/shard_map/ppermute | solution.py:17
  27.5 1218.9 %copy-start.9 = (bf16[16,512]{1,0:T(8,128)(2,1)S(1)}, bf16[16,512]{1,0:T(8,128)(2,1)}, u32[]{:S(2)}) copy-start(bf16[16,512]{1,0:T(8,128)(2,1)} %param.21) | copy-start | bytes 49156
  1250.6 39.8 %collective-permute-start.2 = (bf16[5,1,16,512]{3,2,1,0:T(8,128)(2,1)S(1)}, bf16[5,1,16,512]{3,2,1,0:T(8,128)(2,1)S(1)}, u32[]{:S(2)}, u32[]{:S(2)}) collective-permute-start(bf16[5,1,16,512]{3,2,1,0:T(8,128)(2,1)S(1)} %get-tuple-element.17), channel_id=1, source_target_pairs={{0,1},{1,2},{2,3},{3,4},{4,5},{5,6},{6,7},{7,8},{8,9},{9,10},{10,1... | collective-permute-start | bytes 245768 | tf_op jit(solution)/shard_map/ppermute | solution.py:17
  1288.4 10.2 collective-permute-start.3
  1298.6 1.1 copy-start.11
  1299.7 4.9 copy-start.6
  1299.8 4.9 copy-start.8
  1299.8 4.9 copy-start.14
  1308.2 1.2 copy-start.4
  1308.2 1.2 copy-start.10
  1308.7 1.8 copy-start.7
  1308.7 1.8 copy-start.13
where the time goes:
time: 1310 us
  blocking collectives  1220 us (93%)
  starting transfers between devices  53.5 us (4%)
    all_gather x1, blocking collectives, body(): lax.all_gather(own_coarse, ('row', 'col'), axis=0, tiled=True)  1220 us
    ppermute x2, starting transfers between devices, with_halo(): before = lax.ppermute(last, axis, up)  39.7 us
  transfers between devices with their start and end apart: 4, of which 2 were waited for; matrix products, arithmetic and copies ran while one was open for 1% of the time, Pallas kernels for 0%

commit v1 on v0

v1 whole, which is shorter than its diff:
```python
import functools

import jax
import jax.numpy as jnp
from jax import lax
from jax.experimental import pallas as pl
from jax.experimental.pallas import tpu as pltpu
from jax.sharding import Mesh
from jax.sharding import PartitionSpec as P

epsilon = 1e-05
AXES = ("y", "zh", "core", "x", "zl")
SIZES = (4, 4, 2, 4, 4)
NEAR = ("zh", "core", "zl")
FAR = ("y", "x")
BF = jnp.bfloat16
F32 = jnp.float32
BLOCK = 256


def dot(a, b):
    return jnp.dot(a, b, preferred_element_type=F32)


def column(row):
    return jnp.transpose(jnp.broadcast_to(row, (128, 128)))


def silu(x):
    half = 0.5 * x
    return half + half * jnp.tanh(half)


def layer_norm(values):
    centred = values - jnp.mean(values, axis=-1, keepdims=True)
    second = jnp.mean(centred * centred, axis=-1, keepdims=True)
    return centred * lax.rsqrt(second + epsilon)


def own_kernel(row_ref, nodes_ref, own_ref, message_ref):
    lanes = lax.broadcasted_iota(jnp.int32, (16, 128), 1)
    chosen = (lanes == row_ref[0]).astype(F32).astype(BF)
    own = dot(chosen, nodes_ref[...])
    own_ref[...] = own.astype(BF)
    rows = jnp.concatenate([own[0:1, 128 * k : 128 * k + 128] for k in range(4)], axis=0)
    message_ref[...] = jnp.broadcast_to(rows.astype(BF)[None], (32, 4, 128))


def pick_kernel(send_ref, nodes_ref, down_ref, up_ref, side_ref):
    lanes = lax.broadcasted_iota(jnp.int32, (128, 128), 1)
    chosen = (column(send_ref[...]) == lanes).astype(F32).astype(BF)
    picked = dot(chosen, nodes_ref[...]).astype(BF)
    up_ref[...] = picked[0:48, :]
    side_ref[...] = picked[48:80, :]
    down_ref[...] = picked[80:128, :]


def onehot(ids, width):
    lanes = lax.broadcasted_iota(jnp.int32, ids.shape, 1)
    parts = [(ids == lanes + 128 * k).astype(F32).astype(BF) for k in range(width // 128)]
    return jnp.concatenate(parts, axis=1)


def place(c):
    return (c & 0x180) | ((c & 0xC) << 3) | ((c & 0x70) >> 2) | (c & 3)


def layer_kernel(row_ref, *refs):
    given, out_ref = refs[:NUM], refs[NUM]
    held, (table, summed_ref, sems) = refs[NUM + 1 : 2 * NUM + 1], refs[2 * NUM + 1 :]
    copies = {}
    for i, name in enumerate(NAMES):
        parts = 4 if name == "edges" else 1
        depth = held[i].shape[0] // parts
        copies[name] = []
        for b in range(parts):
            rows = pl.ds(depth * b, depth)
            sem = sems.at[NUM + b if parts > 1 else i]
            copies[name].append(pltpu.make_async_copy(given[i].at[rows], held[i].at[rows], sem))
    for name in NAMES:
        for copy in copies[name]:
            copy.start()

    def got(name, part=0):
        copies[name][part].wait()
        return held[NAMES.index(name)]

    senders = got("senders")[...]
    csenders = got("csenders")[...]
    degrees = column(got("degrees")[...])
    nodes_ref = got("nodes")
    receiver = dot(nodes_ref[...], got("w_receiver")[...])
    crecv = dot(got("own")[...], held[NAMES.index("w_receiver")][...])
    w_edge = got("w_edge")
    edges = held[NAMES.index("edges")]
    cedges = got("cedges")
    wide = lax.broadcasted_iota(jnp.int32, (32, BLOCK), 1)
    node = lax.broadcasted_iota(jnp.int32, (32, BLOCK), 0)
    spots = jnp.where(senders < 256, -1, place(senders - 256))
    pres, nears, fars, uses, aggs = [], [], [], [], []
    for b in range(4):
        got("edges", b)
        rows = slice(BLOCK * b, BLOCK * b + BLOCK)
        before = dot(edges[rows, :], w_edge[...])
        own = receiver[32 * b : 32 * b + 32, :]
        before = before + jnp.broadcast_to(own[:, None, :], (32, 8, 512)).reshape(BLOCK, 512)
        ids = [column(senders[2 * b + i : 2 * b + i + 1, :]) for i in range(2)]
        nears.append(onehot(jnp.concatenate(ids, axis=0), 256))
        ids = [column(spots[2 * b + i : 2 * b + i + 1, :]) for i in range(2)]
        if b == 3:
            before = jnp.concatenate([before, dot(cedges[...], w_edge[...]) + crecv], axis=0)
            ids.append(column(place(csenders))[:16])
        fars.append(onehot(jnp.concatenate(ids, axis=0), 512))
        pres.append(before)
        deg = degrees[32 * b : 32 * b + 32, :]
        deg = jnp.concatenate([deg, deg], axis=1)
        used = (((wide >> 3) == node) & ((wide & 7) < deg)).astype(F32).astype(BF)
        uses.append(used)
        aggs.append(dot(used, edges[rows, :]))

    table[0:128, :] = nodes_ref[...]
    left, right, above, below = got("left"), got("right"), got("above"), got("below")
    for t, (ref, first) in enumerate(
        ((left, 0), (above, 16), (right, 0), (left, 16), (right, 16), (left, 32), (below, 16), (right, 32))
    ):
        table[128 + 16 * t : 144 + 16 * t, :] = ref[first : first + 16, :]
    coarse = got("coarse")
    w_sender = got("w_sender")
    w_message = got("w_message")
    partial = None
    for b in range(4):
        sender = dot(fars[b], coarse[...])
        near = dot(nears[b], table[...])
        if b == 3:
            near = jnp.concatenate([near, jnp.zeros((16, 512), F32)], axis=0)
        sender = (sender + near).astype(BF)
        before = pres[b] + dot(sender, w_sender[...])
        hidden = silu(before).astype(BF)
        message = layer_norm(dot(hidden, w_message[...]))
        high = message[:BLOCK].astype(BF)
        low = (message[:BLOCK] - high.astype(F32)).astype(BF)
        summed_ref[32 * b : 32 * b + 32, :] = aggs[b] + dot(uses[b], high) + dot(uses[b], low)
        if b == 3:
            updated = cedges[...].astype(F32) + message[BLOCK:]
            partial = jnp.sum(updated, axis=0, keepdims=True)
    node_pre = dot(nodes_ref[...], got("w_node")[...])
    owner = lax.broadcasted_iota(jnp.int32, (128, 1), 0) == row_ref[0]
    summed = summed_ref[...] + jnp.where(owner, partial, jnp.zeros_like(partial))
    hidden = silu(node_pre + dot(summed.astype(BF), got("w_gather")[...])).astype(BF)
    result = nodes_ref[...].astype(F32) + layer_norm(dot(hidden, got("w_node_out")[...]))
    out_ref[...] = result.astype(BF)


NAMES = (
    "senders",
    "csenders",
    "degrees",
    "nodes",
    "w_receiver",
    "own",
    "w_edge",
    "edges",
    "cedges",
    "above",
    "left",
    "right",
    "below",
    "coarse",
    "w_sender",
    "w_message",
    "w_node",
    "w_gather",
    "w_node_out",
)
NUM = len(NAMES)


VMEM = pl.BlockSpec(memory_space=pltpu.VMEM)
SMEM = pl.BlockSpec(memory_space=pltpu.SMEM)
ANY = pl.BlockSpec(memory_space=pl.ANY)


def call(kernel, ins, outs, cost, scratch=(), limit=8):
    return pl.pallas_call(
        kernel,
        in_specs=ins,
        out_specs=[VMEM] * len(outs),
        out_shape=[jax.ShapeDtypeStruct(*o) for o in outs],
        scratch_shapes=scratch,
        cost_estimate=pl.CostEstimate(flops=cost, bytes_accessed=cost // 500, transcendentals=0),
        compiler_params=pltpu.CompilerParams(vmem_limit_bytes=limit * 2**20),
    )


def ring(axis_of, step):
    pairs = []
    for flat in range(512):
        r, c = divmod(flat, 16)
        if axis_of == "row":
            r = (r + step) % 32
        else:
            c = (c + step) % 16
        pairs.append((flat, r * 16 + c))
    return pairs


def body(
    node_latents,
    fine_edges,
    fine_senders,
    degrees,
    send_list,
    coarse_row,
    coarse_edges,
    coarse_senders,
    w_edge,
    w_sender,
    w_receiver,
    w_message,
    w_node,
    w_gather,
    w_node_out,
):
    own, message = call(
        own_kernel, [SMEM, VMEM], [((16, 512), BF), ((32, 4, 128), BF)], 2 * 16 * 128 * 512
    )(coarse_row, node_latents)
    coarse = lax.all_to_all(message, NEAR, 0, 0).reshape(1, 32, 512)
    later, _ = lax.optimization_barrier((send_list, message))
    down, up, side = call(
        pick_kernel,
        [VMEM, VMEM],
        [((48, 512), BF), ((48, 512), BF), ((32, 512), BF)],
        2 * 4000 * 512 * 512,
    )(later.reshape(1, 128), node_latents)
    above = lax.ppermute(down, AXES, ring("row", 1))
    below = lax.ppermute(up, AXES, ring("row", -1))
    coarse = lax.all_to_all(jnp.broadcast_to(coarse, (16, 32, 512)), FAR, 0, 0).reshape(512, 512)
    right = jnp.concatenate([above[32:], side[16:], below[32:]], axis=0)
    left = jnp.concatenate([above[:16], side[:16], below[:16]], axis=0)
    from_left = lax.ppermute(right, AXES, ring("col", 1))
    from_right = lax.ppermute(left, AXES, ring("col", -1))

    csenders = jnp.pad(coarse_senders.reshape(1, 16), ((0, 0), (0, 112)))
    given = dict(
        senders=fine_senders.reshape(8, 128),
        csenders=csenders,
        degrees=degrees.reshape(1, 128),
        nodes=node_latents,
        w_receiver=w_receiver,
        own=own,
        w_edge=w_edge,
        edges=fine_edges,
        cedges=coarse_edges,
        above=above,
        left=from_left,
        right=from_right,
        below=below,
        coarse=coarse,
        w_sender=w_sender,
        w_message=w_message,
        w_node=w_node,
        w_gather=w_gather,
        w_node_out=w_node_out,
    )
    (out,) = call(
        layer_kernel,
        [SMEM] + [ANY] * NUM,
        [((128, 512), BF)],
        2 * 7000 * 512 * 512,
        [pltpu.VMEM(given[name].shape, given[name].dtype) for name in NAMES]
        + [
            pltpu.VMEM((256, 512), BF),
            pltpu.VMEM((128, 512), F32),
            pltpu.SemaphoreType.DMA((NUM + 4,)),
        ],
        limit=56,
    )(coarse_row, *[given[name] for name in NAMES])
    return out


def solution(mesh):
    fine = Mesh(mesh.devices.reshape(SIZES), AXES)
    rows, lists = P(AXES, None), P(AXES)
    placed = (rows, rows, lists, lists, lists, lists, rows, lists) + (P(),) * 7
    return jax.shard_map(body, mesh=fine, in_specs=placed, out_specs=rows, check_vma=False)
```

time: 1310 us -> 67.9 us (0.05)
  the two profiles are of different devices: /device:TPU:102 before, /device:TPU:8 now
where the time goes in v1:
time: 67.9 us; the launch traced here: 67.5 us
  starting transfers between devices  42.8 us (63%)
  Pallas kernels  9.8 us (14%)
  waiting for transfers between devices  9.17 us (14%)
  local copies, waits for them, and re-layouts  4.92 us (7%)
  between operations  0.81 us (1%)
    all_to_all x1, starting transfers between devices, body(): coarse = lax.all_to_all(message, NEAR, 0, 0).reshape(1, 32, 512)  15.5 us
    pallas_call x1, Pallas kernels, body(): call(layer_kernel, [SMEM] + [ANY] * NUM, [((128, 512), BF)], 2 * 7000 * 5...  8.82 us
    ppermute x1, starting transfers between devices, body(): below = lax.ppermute(up, AXES, ring('row', -1))  8.19 us
    ppermute x1, starting transfers between devices, body(): from_right = lax.ppermute(left, AXES, ring('col', -1))  7.62 us
    ppermute x1, waiting for transfers between devices, body(): from_left = lax.ppermute(right, AXES, ring('col', 1))  7.46 us
    all_to_all x1, starting transfers between devices, body(): lax.all_to_all(jnp.broadcast_to(coarse, (16, 32, 512)), FAR, 0, 0)  7.39 us
    unnamed x21, local copies, waits for them, and re-layouts  3.56 us
    ppermute x1, starting transfers between devices, body(): above = lax.ppermute(down, AXES, ring('row', 1))  2.18 us
  transfers between devices with their start and end apart: 6, of which 2 were waited for; matrix products, arithmetic and copies ran while one was open for 2% of the time, Pallas kernels for 0%

profile of v1, /device:TPU:8, one launch (start us, length us, event | category | flops | bytes accessed | tf_op | source)
XLA Modules:
  0.0 67.5 jit_solution(3709389999509676243)
XLA Ops:
  0.7 0.0 copy-start
  0.7 0.9 %copy-done = bf16[128,512]{1,0:T(8,128)(2,1)S(1)} copy-done((bf16[128,512]{1,0:T(8,128)(2,1)S(1)}, bf16[128,512]{1,0:T(8,128)(2,1)}, u32[]{:S(2)}) %copy-start) | copy-done | bytes 131096
  1.6 0.8 %shard_map.145 = (bf16[16,512]{1,0:T(8,128)(2,1)S(1)}, bf16[32,4,128]{2,1,0:T(4,128)(2,1)}) custom-call(s32[1]{0:T(128)S(6)} %copy.19.row_ref, bf16[128,512]{1,0:T(8,128)(2,1)S(1)} %copy-done), custom_call_target="tpu_custom_call" | custom-call | flops 2097152 | bytes 4194 | tf_op jit(solution)/shard_map/pallas_call | solution.py:224
  2.3 0.6 copy-done.2
  2.9 15.5 %all-to-all-start = ((bf16[32,4,128]{2,1,0:T(4,128)(2,1)}), bf16[32,4,128]{2,1,0:T(4,128)(2,1)S(1)}, u32[]{:S(2)}, u32[]{:S(2)}) async-start(bf16[32,4,128]{2,1,0:T(4,128)(2,1)} %get-tuple-element.12), calls=%async_computation | async-start | bytes 65536 | tf_op jit(solution)/shard_map/all_to_all | solution.py:227
  18.4 0.0 copy-start.3
  18.4 0.6 copy-done.3
  19.1 0.2 shard_map.146
  19.3 2.2 %collective-permute-start = (bf16[48,512]{1,0:T(8,128)(2,1)S(1)}, bf16[48,512]{1,0:T(8,128)(2,1)S(1)}, u32[]{:S(2)}, u32[]{:S(2)}) collective-permute-start(bf16[48,512]{1,0:T(8,128)(2,1)S(1)} %get-tuple-element.14), channel_id=1, source_target_pairs={{0,16},{1,17},{2,18},{3,19},{4,20},{5,21},{6,22},{7,23},{8,24},{9,... | collective-permute-start | bytes 147464 | tf_op jit(solution)/shard_map/ppermute | solution.py:235
  21.5 8.2 %collective-permute-start.1 = (bf16[48,512]{1,0:T(8,128)(2,1)S(1)}, bf16[48,512]{1,0:T(8,128)(2,1)S(1)}, u32[]{:S(2)}, u32[]{:S(2)}) collective-permute-start(bf16[48,512]{1,0:T(8,128)(2,1)S(1)} %get-tuple-element.16), channel_id=1, source_target_pairs={{0,496},{1,497},{2,498},{3,499},{4,500},{5,501},{6,502},{7,503},{8... | collective-permute-start | bytes 147464 | tf_op jit(solution)/shard_map/ppermute | solution.py:236
  29.7 0.0 collective-permute-done.refs_9_
  29.7 1.7 %all-to-all-done = bf16[32,4,128]{2,1,0:T(4,128)(2,1)S(1)} async-done(((bf16[32,4,128]{2,1,0:T(4,128)(2,1)}), bf16[32,4,128]{2,1,0:T(4,128)(2,1)S(1)}, u32[]{:S(2)}, u32[]{:S(2)}) %all-to-all-start) | async-done | bytes 32800 | tf_op jit(solution)/shard_map/all_to_all | solution.py:227
  31.4 0.9 %broadcast_in_dim.8 = bf16[16,32,512]{2,1,0:T(8,128)(2,1)} broadcast(bf16[32,512]{1,0:T(8,128)(2,1)S(1)} %bitcast.11), dimensions={1,2} | broadcast | bytes 557056 | tf_op jit(solution)/shard_map/broadcast_in_dim | solution.py:237
  32.3 7.4 %all-to-all-start.1 = ((bf16[16,32,512]{2,1,0:T(8,128)(2,1)}), bf16[16,32,512]{2,1,0:T(8,128)(2,1)S(1)}, u32[]{:S(2)}, u32[]{:S(2)}) async-start(bf16[16,32,512]{2,1,0:T(8,128)(2,1)} %broadcast_in_dim.8), calls=%async_computation.1 | async-start | bytes 1048576 | tf_op jit(solution)/shard_map/all_to_all | solution.py:237
  39.7 0.0 collective-permute-done.1.refs_12_
  39.7 0.6 copy-done.6
  40.3 7.6 %collective-permute-start.3 = (bf16[48,512]{1,0:T(8,128)(2,1)S(1)}, bf16[48,512]{1,0:T(8,128)(2,1)S(1)}, u32[]{:S(2)}, u32[]{:S(2)}) collective-permute-start(bf16[48,512]{1,0:T(8,128)(2,1)S(1)} %pad_maximum_fusion.1), channel_id=1, source_target_pairs={{0,15},{1,0},{2,1},{3,2},{4,3},{5,4},{6,5},{7,6},{8,7},{9,8},{10,9... | collective-permute-start | bytes 147464 | tf_op jit(solution)/shard_map/ppermute | solution.py:241
  47.9 0.0 copy-start.9
  47.9 1.9 %collective-permute-start.2 = (bf16[48,512]{1,0:T(8,128)(2,1)S(1)}, bf16[48,512]{1,0:T(8,128)(2,1)S(1)}, u32[]{:S(2)}, u32[]{:S(2)}) collective-permute-start(bf16[48,512]{1,0:T(8,128)(2,1)S(1)} %pad_maximum_fusion), channel_id=1, source_target_pairs={{0,1},{1,2},{2,3},{3,4},{4,5},{5,6},{6,7},{7,8},{8,9},{9,10},{10,1... | collective-permute-start | bytes 147464 | tf_op jit(solution)/shard_map/ppermute | solution.py:240
  49.9 0.5 pad.4.refs_1_
  50.4 7.5 %collective-permute-done.2.refs_10_ = bf16[48,512]{1,0:T(8,128)(2,1)S(1)} collective-permute-done((bf16[48,512]{1,0:T(8,128)(2,1)S(1)}, bf16[48,512]{1,0:T(8,128)(2,1)S(1)}, u32[]{:S(2)}, u32[]{:S(2)}) %collective-permute-start.2) | collective-permute-done | bytes 49184 | tf_op jit(solution)/shard_map/ppermute | solution.py:240
  57.9 0.6 copy-done.8
  58.5 0.2 copy-done.4
  58.7 8.8 %shard_map.147 = bf16[128,512]{1,0:T(8,128)(2,1)} custom-call(s32[1]{0:T(128)S(6)} %copy.19.row_ref, s32[8,128]{1,0:T(8,128)} %bitcast.13, s32[1,128]{1,0:T(1,128)} %pad.4.refs_1_, s32[1,128]{1,0:T(1,128)} %bitcast.15, bf16[128,512]{1,0:T(8,128)(2,1)} %refs_3_.1, bf16[512,512]{1,0:T(8,128)(2,1)} %refs_4_.1, bf16[16,512]{1,0:T(8,128)(2,1)} %copy-done.2, ...), custom_call_target="tpu_custom_call" | custom-call | flops 3670016000 | bytes 7340032 | tf_op jit(solution)/shard_map/pallas_call | solution.py:265
  (19 shorter events, 0.1 us)
Async XLA Ops:
  0.7 0.9 %copy-start = (bf16[128,512]{1,0:T(8,128)(2,1)S(1)}, bf16[128,512]{1,0:T(8,128)(2,1)}, u32[]{:S(2)}) copy-start(bf16[128,512]{1,0:T(8,128)(2,1)} %refs_3_.1) | copy-start | bytes 393220
  1.6 16.9 %copy-start.1 = (bf16[128,512]{1,0:T(8,128)(2,1)S(1)}, bf16[128,512]{1,0:T(8,128)(2,1)}, u32[]{:S(2)}) copy-start(bf16[128,512]{1,0:T(8,128)(2,1)} %refs_3_.1) | copy-start | bytes 393220
  2.3 0.6 copy-start.2
  2.9 28.5 %all-to-all-start = ((bf16[32,4,128]{2,1,0:T(4,128)(2,1)}), bf16[32,4,128]{2,1,0:T(4,128)(2,1)S(1)}, u32[]{:S(2)}, u32[]{:S(2)}) async-start(bf16[32,4,128]{2,1,0:T(4,128)(2,1)} %get-tuple-element.12), calls=%async_computation | async-start | bytes 65536 | tf_op jit(solution)/shard_map/all_to_all | solution.py:227
  18.4 0.7 copy-start.3
  19.3 10.4 %collective-permute-start = (bf16[48,512]{1,0:T(8,128)(2,1)S(1)}, bf16[48,512]{1,0:T(8,128)(2,1)S(1)}, u32[]{:S(2)}, u32[]{:S(2)}) collective-permute-start(bf16[48,512]{1,0:T(8,128)(2,1)S(1)} %get-tuple-element.14), channel_id=1, source_target_pairs={{0,16},{1,17},{2,18},{3,19},{4,20},{5,21},{6,22},{7,23},{8,24},{9,... | collective-permute-start | bytes 147464 | tf_op jit(solution)/shard_map/ppermute | solution.py:235
  21.5 18.2 %collective-permute-start.1 = (bf16[48,512]{1,0:T(8,128)(2,1)S(1)}, bf16[48,512]{1,0:T(8,128)(2,1)S(1)}, u32[]{:S(2)}, u32[]{:S(2)}) collective-permute-start(bf16[48,512]{1,0:T(8,128)(2,1)S(1)} %get-tuple-element.16), channel_id=1, source_target_pairs={{0,496},{1,497},{2,498},{3,499},{4,500},{5,501},{6,502},{7,503},{8... | collective-permute-start | bytes 147464 | tf_op jit(solution)/shard_map/ppermute | solution.py:236
  29.7 1.7 %copy-start.5 = (bf16[48,512]{1,0:T(8,128)(2,1)}, bf16[48,512]{1,0:T(8,128)(2,1)S(1)}, u32[]{:S(2)}) copy-start(bf16[48,512]{1,0:T(8,128)(2,1)S(1)} %collective-permute-done.refs_9_) | copy-start | bytes 147460
  32.3 25.6 %all-to-all-start.1 = ((bf16[16,32,512]{2,1,0:T(8,128)(2,1)}), bf16[16,32,512]{2,1,0:T(8,128)(2,1)S(1)}, u32[]{:S(2)}, u32[]{:S(2)}) async-start(bf16[16,32,512]{2,1,0:T(8,128)(2,1)} %broadcast_in_dim.8), calls=%async_computation.1 | async-start | bytes 1048576 | tf_op jit(solution)/shard_map/all_to_all | solution.py:237
  39.7 0.6 copy-start.6
  40.3 10.1 %collective-permute-start.3 = (bf16[48,512]{1,0:T(8,128)(2,1)S(1)}, bf16[48,512]{1,0:T(8,128)(2,1)S(1)}, u32[]{:S(2)}, u32[]{:S(2)}) collective-permute-start(bf16[48,512]{1,0:T(8,128)(2,1)S(1)} %pad_maximum_fusion.1), channel_id=1, source_target_pairs={{0,15},{1,0},{2,1},{3,2},{4,3},{5,4},{6,5},{7,6},{8,7},{9,8},{10,9... | collective-permute-start | bytes 147464 | tf_op jit(solution)/shard_map/ppermute | solution.py:241
  47.9 1.9 %copy-start.9 = (s32[16]{0:T(128)S(1)}, s32[16]{0:T(128)}, u32[]{:S(2)}) copy-start(s32[16]{0:T(128)} %param.22) | copy-start | bytes 196
  47.9 9.9 %collective-permute-start.2 = (bf16[48,512]{1,0:T(8,128)(2,1)S(1)}, bf16[48,512]{1,0:T(8,128)(2,1)S(1)}, u32[]{:S(2)}, u32[]{:S(2)}) collective-permute-start(bf16[48,512]{1,0:T(8,128)(2,1)S(1)} %pad_maximum_fusion), channel_id=1, source_target_pairs={{0,1},{1,2},{2,3},{3,4},{4,5},{5,6},{6,7},{7,8},{8,9},{9,10},{10,1... | collective-permute-start | bytes 147464 | tf_op jit(solution)/shard_map/ppermute | solution.py:240
  50.4 7.5 %copy-start.7 = (bf16[48,512]{1,0:T(8,128)(2,1)}, bf16[48,512]{1,0:T(8,128)(2,1)S(1)}, u32[]{:S(2)}) copy-start(bf16[48,512]{1,0:T(8,128)(2,1)S(1)} %collective-permute-done.3.refs_11_) | copy-start | bytes 147460
  57.8 0.6 copy-start.8
  57.8 0.8 %copy-start.4 = (bf16[16,32,512]{2,1,0:T(8,128)(2,1)}, bf16[16,32,512]{2,1,0:T(8,128)(2,1)S(1)}, u32[]{:S(2)}) copy-start(bf16[16,32,512]{2,1,0:T(8,128)(2,1)S(1)} %all-to-all-done.1) | copy-start | bytes 1572868

commit v2 on v1

v2 whole, which is shorter than its diff:
```python
import functools

import jax
import jax.numpy as jnp
from jax import lax
from jax.experimental import pallas as pl
from jax.experimental.pallas import tpu as pltpu
from jax.sharding import Mesh
from jax.sharding import PartitionSpec as P

epsilon = 1e-05
AXES = ("y", "zh", "core", "x", "zl")
SIZES = (4, 4, 2, 4, 4)
NEAR = ("zh", "core", "zl")
FAR = ("y", "x")
BF = jnp.bfloat16
F32 = jnp.float32
BLOCK = 256


def dot(a, b):
    return jnp.dot(a, b, preferred_element_type=F32)


def column(row):
    return jnp.transpose(jnp.broadcast_to(row, (128, 128)))


def silu(x):
    half = 0.5 * x
    return half + half * jnp.tanh(half)


def layer_norm(values):
    centred = values - jnp.mean(values, axis=-1, keepdims=True)
    second = jnp.mean(centred * centred, axis=-1, keepdims=True)
    return centred * lax.rsqrt(second + epsilon)


def pick_kernel(
    row_ref, odd_ref, send_ref, nodes_ref, first_ref, second_ref, side_ref, own_ref, message_ref
):
    lanes = lax.broadcasted_iota(jnp.int32, (128, 128), 1)
    chosen = (column(send_ref[...]) == lanes).astype(F32).astype(BF)
    picked = dot(chosen, nodes_ref[...])
    odd = odd_ref[0] == 1
    first_ref[...] = jnp.where(odd, picked[0:48, :], picked[80:128, :]).astype(BF)
    second_ref[...] = jnp.where(odd, picked[80:128, :], picked[0:48, :]).astype(BF)
    side_ref[...] = picked[48:80, :].astype(BF)
    chosen = (lanes[:16] == row_ref[0]).astype(F32).astype(BF)
    own = dot(chosen, nodes_ref[...])
    own_ref[...] = own.astype(BF)
    rows = jnp.concatenate([own[0:1, 128 * k : 128 * k + 128] for k in range(4)], axis=0)
    message_ref[...] = jnp.broadcast_to(rows.astype(BF)[None], (32, 4, 128))


def onehot(ids, width):
    lanes = lax.broadcasted_iota(jnp.int32, ids.shape, 1)
    parts = [(ids == lanes + 128 * k).astype(F32).astype(BF) for k in range(width // 128)]
    return jnp.concatenate(parts, axis=1)


def place(c):
    return (c & 0x180) | ((c & 0xC) << 3) | ((c & 0x70) >> 2) | (c & 3)


NAMES = (
    "senders",
    "nodes",
    "w_receiver",
    "w_edge",
    "edges",
    "coarse",
    "degrees",
    "own",
    "cedges",
    "csenders",
    "w_node",
)
NUM = len(NAMES)


def local_kernel(*refs):
    given, held = refs[:NUM], refs[NUM + 6 : 2 * NUM + 6]
    pre_ref, far_ref, near_ref, use_ref, agg_ref, node_pre_ref = refs[NUM : NUM + 6]
    (sems,) = refs[2 * NUM + 6 :]
    copies = {}
    for i, name in enumerate(NAMES):
        parts = 4 if name == "edges" else 1
        depth = held[i].shape[0] // parts
        copies[name] = []
        for b in range(parts):
            rows = pl.ds(depth * b, depth)
            sem = sems.at[NUM + b if parts > 1 else i]
            copies[name].append(pltpu.make_async_copy(given[i].at[rows], held[i].at[rows], sem))
            copies[name][b].start()

    def got(name, part=0):
        copies[name][part].wait()
        return held[NAMES.index(name)]

    senders_ref, nodes_ref = got("senders"), got("nodes")
    w_receiver_ref, w_edge_ref = got("w_receiver"), got("w_edge")
    edges_ref = held[NAMES.index("edges")]
    nodes = nodes_ref[...]
    receiver = dot(nodes, w_receiver_ref[...])
    senders = senders_ref[...]
    spots = jnp.where(senders < 256, -1, place(senders - 256))
    wide = lax.broadcasted_iota(jnp.int32, (32, BLOCK), 1)
    node = lax.broadcasted_iota(jnp.int32, (32, BLOCK), 0)
    for b in range(4):
        rows = slice(BLOCK * b, BLOCK * b + BLOCK)
        got("edges", b)
        before = dot(edges_ref[rows, :], w_edge_ref[...])
        own = receiver[32 * b : 32 * b + 32, :]
        pre_ref[rows, :] = before + jnp.broadcast_to(own[:, None, :], (32, 8, 512)).reshape(BLOCK, 512)
    coarse_ref = got("coarse")
    degrees = column(got("degrees")[...])
    for b in range(4):
        rows = slice(BLOCK * b, BLOCK * b + BLOCK)
        ids = [column(senders[2 * b + i : 2 * b + i + 1, :]) for i in range(2)]
        near_ref[rows, :] = onehot(jnp.concatenate(ids, axis=0), 256)
        ids = [column(spots[2 * b + i : 2 * b + i + 1, :]) for i in range(2)]
        chosen = onehot(jnp.concatenate(ids, axis=0), 512)
        far_ref[rows, :] = dot(chosen, coarse_ref[...]).astype(BF)
        deg = degrees[32 * b : 32 * b + 32, :]
        deg = jnp.concatenate([deg, deg], axis=1)
        used = (((wide >> 3) == node) & ((wide & 7) < deg)).astype(F32).astype(BF)
        use_ref[32 * b : 32 * b + 32, :] = used
        agg_ref[32 * b : 32 * b + 32, :] = dot(used, edges_ref[rows, :])
    own_ref, cedges_ref, csenders_ref = got("own"), got("cedges"), got("csenders")
    coarse = dot(cedges_ref[...], w_edge_ref[...])
    pre_ref[1024:1040, :] = coarse + dot(own_ref[...], w_receiver_ref[...])
    chosen = onehot(column(place(csenders_ref[...]))[:16], 512)
    far_ref[1024:1040, :] = dot(chosen, coarse_ref[...]).astype(BF)
    node_pre_ref[...] = dot(nodes, got("w_node")[...])


def final_kernel(
    row_ref,
    odd_ref,
    pre_ref,
    far_ref,
    near_ref,
    use_ref,
    agg_ref,
    node_pre_ref,
    nodes_ref,
    cedges_ref,
    row_first_ref,
    row_second_ref,
    col_first_ref,
    col_second_ref,
    w_sender_ref,
    w_message_ref,
    w_gather_ref,
    w_node_out_ref,
    out_ref,
    table,
    summed_ref,
):
    def fill(left, right, above, below):
        spots = (
            (left, 0),
            (above, 16),
            (right, 0),
            (left, 16),
            (right, 16),
            (left, 32),
            (below, 16),
            (right, 32),
        )
        for t, (ref, first) in enumerate(spots):
            table[128 + 16 * t : 144 + 16 * t, :] = ref[first : first + 16, :]

    table[0:128, :] = nodes_ref[...]
    for odd_row in range(2):
        for odd_col in range(2):
            above, below = (row_first_ref, row_second_ref) if odd_row else (row_second_ref, row_first_ref)
            left, right = (col_first_ref, col_second_ref) if odd_col else (col_second_ref, col_first_ref)

            @pl.when((odd_ref[0] == odd_row) & (odd_ref[1] == odd_col))
            def _(left=left, right=right, above=above, below=below):
                fill(left, right, above, below)

    partial = None
    for b in range(4):
        rows = slice(BLOCK * b, BLOCK * b + BLOCK)
        sender = dot(near_ref[rows, :], table[...]).astype(BF) + far_ref[rows, :]
        if b == 3:
            rows = slice(BLOCK * b, BLOCK * b + BLOCK + 16)
            sender = jnp.concatenate([sender, far_ref[1024:1040, :]], axis=0)
        before = pre_ref[rows, :] + dot(sender, w_sender_ref[...])
        hidden = silu(before).astype(BF)
        message = layer_norm(dot(hidden, w_message_ref[...]))
        used = use_ref[32 * b : 32 * b + 32, :]
        high = message[:BLOCK].astype(BF)
        low = (message[:BLOCK] - high.astype(F32)).astype(BF)
        summed_ref[32 * b : 32 * b + 32, :] = (
            agg_ref[32 * b : 32 * b + 32, :] + dot(used, high) + dot(used, low)
        )
        if b == 3:
            updated = cedges_ref[...].astype(F32) + message[BLOCK:]
            partial = jnp.sum(updated, axis=0, keepdims=True)
    owner = lax.broadcasted_iota(jnp.int32, (128, 1), 0) == row_ref[0]
    summed = summed_ref[...] + jnp.where(owner, partial, jnp.zeros_like(partial))
    hidden = silu(node_pre_ref[...] + dot(summed.astype(BF), w_gather_ref[...])).astype(BF)
    result = nodes_ref[...].astype(F32) + layer_norm(dot(hidden, w_node_out_ref[...]))
    out_ref[...] = result.astype(BF)


VMEM = pl.BlockSpec(memory_space=pltpu.VMEM)
SMEM = pl.BlockSpec(memory_space=pltpu.SMEM)
HBM = pl.BlockSpec(memory_space=pltpu.HBM)
ANY = pl.BlockSpec(memory_space=pl.ANY)


def call(kernel, ins, outs, cost, scratch=(), limit=8):
    return pl.pallas_call(
        kernel,
        in_specs=ins,
        out_specs=[VMEM] * len(outs),
        out_shape=[jax.ShapeDtypeStruct(*o) for o in outs],
        scratch_shapes=scratch,
        cost_estimate=pl.CostEstimate(flops=cost, bytes_accessed=cost // 500, transcendentals=0),
        compiler_params=pltpu.CompilerParams(vmem_limit_bytes=limit * 2**20),
    )


def swap(axis, odd):
    pairs = []
    for flat in range(512):
        at = list(divmod(flat, 16))
        step = 1 if at[axis] % 2 == odd else -1
        at[axis] = (at[axis] + step) % (32, 16)[axis]
        pairs.append((flat, at[0] * 16 + at[1]))
    return pairs


def body(
    node_latents,
    fine_edges,
    fine_senders,
    degrees,
    send_list,
    coarse_row,
    coarse_edges,
    coarse_senders,
    w_edge,
    w_sender,
    w_receiver,
    w_message,
    w_node,
    w_gather,
    w_node_out,
):
    odd = jnp.stack([lax.axis_index("core"), lax.axis_index("zl") % 2]).astype(jnp.int32)
    first, second, side, own, message = call(
        pick_kernel,
        [SMEM, SMEM, VMEM, VMEM],
        [
            ((48, 512), BF),
            ((48, 512), BF),
            ((32, 512), BF),
            ((16, 512), BF),
            ((32, 4, 128), BF),
        ],
        2 * 144 * 128 * 512,
    )(coarse_row, odd, send_list.reshape(1, 128), node_latents)
    z_rows = lax.all_to_all(message, NEAR, 0, 0)
    row_first = lax.ppermute(first, AXES, swap(0, 0))
    row_second = lax.ppermute(second, AXES, swap(0, 1))
    above = jnp.where(odd[0] == 1, row_first, row_second)
    below = jnp.where(odd[0] == 1, row_second, row_first)
    right = jnp.concatenate([above[32:], side[16:], below[32:]], axis=0)
    left = jnp.concatenate([above[:16], side[:16], below[:16]], axis=0)
    col_first = lax.ppermute(jnp.where(odd[1] == 1, left, right), AXES, swap(1, 0))
    col_second = lax.ppermute(jnp.where(odd[1] == 1, right, left), AXES, swap(1, 1))
    z_rows = z_rows.reshape(1, 32, 512)
    coarse = lax.all_to_all(jnp.broadcast_to(z_rows, (16, 32, 512)), FAR, 0, 0).reshape(512, 512)
    csenders = jnp.pad(coarse_senders.reshape(1, 16), ((0, 0), (0, 112)))
    given = dict(
        senders=fine_senders.reshape(8, 128),
        csenders=csenders,
        degrees=degrees.reshape(1, 128),
        own=own,
        nodes=node_latents,
        edges=fine_edges,
        cedges=coarse_edges,
        coarse=coarse,
        w_edge=w_edge,
        w_receiver=w_receiver,
        w_node=w_node,
    )
    kept = ("coarse", "own", "senders", "csenders", "degrees")
    pre, far, near, use, agg, node_pre = call(
        local_kernel,
        [ANY if name in kept else HBM for name in NAMES],
        [
            ((1040, 512), F32),
            ((1040, 512), BF),
            ((1024, 256), BF),
            ((128, BLOCK), BF),
            ((128, 512), F32),
            ((128, 512), F32),
        ],
        2 * 3500 * 512 * 512,
        [pltpu.VMEM(given[name].shape, given[name].dtype) for name in NAMES]
        + [pltpu.SemaphoreType.DMA((NUM + 4,))],
        limit=12,
    )(*[given[name] for name in NAMES])
    (out,) = call(
        final_kernel,
        [SMEM, SMEM] + [VMEM] * 16,
        [((128, 512), BF)],
        2 * 5000 * 512 * 512,
        [pltpu.VMEM((256, 512), BF), pltpu.VMEM((128, 512), F32)],
    )(
        coarse_row,
        odd,
        pre,
        far,
        near,
        use,
        agg,
        node_pre,
        node_latents,
        coarse_edges,
        row_first,
        row_second,
        col_first,
        col_second,
        w_sender,
        w_message,
        w_gather,
        w_node_out,
    )
    return out


def solution(mesh):
    fine = Mesh(mesh.devices.reshape(SIZES), AXES)
    rows, lists = P(AXES, None), P(AXES)
    placed = (rows, rows, lists, lists, lists, lists, rows, lists) + (P(),) * 7
    return jax.shard_map(body, mesh=fine, in_specs=placed, out_specs=rows, check_vma=False)
```

time: 67.9 us -> 61.4 us (0.904)
  the two profiles are of different devices: /device:TPU:8 before, /device:TPU:32 now
where the time goes in v2:
time: 61.4 us; the launch traced here: 61 us
  starting transfers between devices  38.6 us (63%)
  Pallas kernels  10.6 us (17%)
  waiting for transfers between devices  6.53 us (11%)
  local copies, waits for them, and re-layouts  4.18 us (7%)
  between operations  0.92 us (1%)
    all_to_all x1, starting transfers between devices, body(): z_rows = lax.all_to_all(message, NEAR, 0, 0)  15.4 us
    ppermute x1, starting transfers between devices, body(): row_second = lax.ppermute(second, AXES, swap(0, 1))  8.84 us
    all_to_all x1, starting transfers between devices, body(): lax.all_to_all(jnp.broadcast_to(z_rows, (16, 32, 512)), FAR, 0, 0)  7.04 us
    all_to_all x1, waiting for transfers between devices, body(): lax.all_to_all(jnp.broadcast_to(z_rows, (16, 32, 512)), FAR, 0, 0)  6.34 us
    pallas_call x1, Pallas kernels, body(): call(final_kernel, [SMEM, SMEM] + [VMEM] * 16, [((128, 512), BF)], 2 * 50...  5.62 us
    pallas_call x1, Pallas kernels, body(): call(local_kernel, [ANY if name in kept else HBM for name in NAMES], [((1...  3.54 us
    ppermute x1, starting transfers between devices, body(): lax.ppermute(jnp.where(odd[1] == 1, left, right), AXES, swap(1, 0))  3.44 us
    unnamed x29, local copies, waits for them, and re-layouts  2.64 us
  transfers between devices with their start and end apart: 6, of which 2 were waited for; matrix products, arithmetic and copies ran while one was open for 3% of the time, Pallas kernels for 6%

profile of v2, /device:TPU:32, one launch (start us, length us, event | category | flops | bytes accessed | tf_op | source)
XLA Modules:
  0.0 61.0 jit_solution(17794343514015595179)
XLA Ops:
  0.7 0.1 pad_add_fusion.odd_ref
  0.8 0.9 %copy-done = bf16[128,512]{1,0:T(8,128)(2,1)S(1)} copy-done((bf16[128,512]{1,0:T(8,128)(2,1)S(1)}, bf16[128,512]{1,0:T(8,128)(2,1)}, u32[]{:S(2)}) %copy-start) | copy-done | bytes 131096
  1.7 0.7 %copy-done.2 = s32[128]{0:T(128)S(1)} copy-done((s32[128]{0:T(128)S(1)}, s32[128]{0:T(128)}, u32[]{:S(2)}) %copy-start.2) | copy-done | bytes 536
  2.4 1.4 %shard_map.145 = (bf16[48,512]{1,0:T(8,128)(2,1)S(1)}, bf16[48,512]{1,0:T(8,128)(2,1)S(1)}, bf16[32,512]{1,0:T(8,128)(2,1)S(1)}, bf16[16,512]{1,0:T(8,128)(2,1)S(1)}, bf16[32,4,128]{2,1,0:T(4,128)(2,1)}) custom-call(s32[1]{0:T(128)S(6)} %copy.19.row_ref, s32[2]{0:T(128)S(1)} %pad_add_fusion.odd_ref, s32[1,128]{1,0:T(1,128)S(1)} %bitcast.12, ...), custom_call_target="tpu_custom_call" | custom-call | flops 18874368 | bytes 37748 | tf_op jit(solution)/shard_map/pallas_call | solution.py:258
  3.8 15.4 %all-to-all-start = ((bf16[32,4,128]{2,1,0:T(4,128)(2,1)}), bf16[32,4,128]{2,1,0:T(4,128)(2,1)S(1)}, u32[]{:S(2)}, u32[]{:S(2)}) async-start(bf16[32,4,128]{2,1,0:T(4,128)(2,1)} %get-tuple-element.16), calls=%async_computation | async-start | bytes 65536 | tf_op jit(solution)/shard_map/all_to_all | solution.py:270
  19.1 2.1 %collective-permute-start = (bf16[48,512]{1,0:T(8,128)(2,1)S(1)}, bf16[48,512]{1,0:T(8,128)(2,1)S(1)}, u32[]{:S(2)}, u32[]{:S(2)}) collective-permute-start(bf16[48,512]{1,0:T(8,128)(2,1)S(1)} %get-tuple-element.24), channel_id=1, source_target_pairs={{0,16},{1,17},{2,18},{3,19},{4,20},{5,21},{6,22},{7,23},{8,24},{9,... | collective-permute-start | bytes 147464 | tf_op jit(solution)/shard_map/ppermute | solution.py:271
  21.2 8.8 %collective-permute-start.1 = (bf16[48,512]{1,0:T(8,128)(2,1)S(1)}, bf16[48,512]{1,0:T(8,128)(2,1)S(1)}, u32[]{:S(2)}, u32[]{:S(2)}) collective-permute-start(bf16[48,512]{1,0:T(8,128)(2,1)S(1)} %get-tuple-element.25), channel_id=1, source_target_pairs={{0,496},{1,497},{2,498},{3,499},{4,500},{5,501},{6,502},{7,503},{8... | collective-permute-start | bytes 147464 | tf_op jit(solution)/shard_map/ppermute | solution.py:272
  30.1 0.7 %pad.4.refs_9_ = s32[1,128]{1,0:T(1,128)S(1)} pad(s32[1,16]{1,0:T(1,128)} %bitcast.17, s32[]{:T(128)} %constant.22.clone.1), padding=0_0x0_112 | pad | bytes 580 | tf_op jit(solution)/shard_map/jit(_pad)/pad | solution.py:281
  30.7 0.2 all-to-all-done
  30.9 0.9 %broadcast_in_dim.8 = bf16[16,32,512]{2,1,0:T(8,128)(2,1)} broadcast(bf16[32,512]{1,0:T(8,128)(2,1)S(1)} %bitcast.15), dimensions={1,2} | broadcast | bytes 557056 | tf_op jit(solution)/shard_map/broadcast_in_dim | solution.py:280
  31.8 7.0 %all-to-all-start.1 = ((bf16[16,32,512]{2,1,0:T(8,128)(2,1)}), bf16[16,32,512]{2,1,0:T(8,128)(2,1)S(1)}, u32[]{:S(2)}, u32[]{:S(2)}) async-start(bf16[16,32,512]{2,1,0:T(8,128)(2,1)} %broadcast_in_dim.8), calls=%async_computation.1 | async-start | bytes 1048576 | tf_op jit(solution)/shard_map/all_to_all | solution.py:280
  38.8 0.0 collective-permute-done.row_first_ref
  38.8 0.0 collective-permute-done.1.row_second_ref
  38.9 3.4 %collective-permute-start.2 = (bf16[48,512]{1,0:T(8,128)(2,1)S(1)}, bf16[48,512]{1,0:T(8,128)(2,1)S(1)}, u32[]{:S(2)}, u32[]{:S(2)}) collective-permute-start(bf16[48,512]{1,0:T(8,128)(2,1)S(1)} %get-tuple-element.28), channel_id=1, source_target_pairs={{0,1},{1,0},{2,3},{3,2},{4,5},{5,4},{6,7},{7,6},{8,9},{9,8},{10,11... | collective-permute-start | bytes 147464 | tf_op jit(solution)/shard_map/ppermute | solution.py:277
  42.4 1.9 %collective-permute-start.3 = (bf16[48,512]{1,0:T(8,128)(2,1)S(1)}, bf16[48,512]{1,0:T(8,128)(2,1)S(1)}, u32[]{:S(2)}, u32[]{:S(2)}) collective-permute-start(bf16[48,512]{1,0:T(8,128)(2,1)S(1)} %get-tuple-element.27), channel_id=1, source_target_pairs={{0,15},{1,2},{2,1},{3,4},{4,3},{5,6},{6,5},{7,8},{8,7},{9,10},{10,... | collective-permute-start | bytes 147464 | tf_op jit(solution)/shard_map/ppermute | solution.py:278
  44.3 6.3 %all-to-all-done.1 = bf16[16,32,512]{2,1,0:T(8,128)(2,1)S(1)} async-done(((bf16[16,32,512]{2,1,0:T(8,128)(2,1)}), bf16[16,32,512]{2,1,0:T(8,128)(2,1)S(1)}, u32[]{:S(2)}, u32[]{:S(2)}) %all-to-all-start.1) | async-done | bytes 524320 | tf_op jit(solution)/shard_map/all_to_all | solution.py:280
  50.6 0.0 copy-done.1
  50.6 0.0 copy-done.3
  50.7 0.0 copy-start.6
  50.7 1.0 %copy-done.6 = bf16[512,512]{1,0:T(8,128)(2,1)S(1)} copy-done((bf16[512,512]{1,0:T(8,128)(2,1)S(1)}, bf16[512,512]{1,0:T(8,128)(2,1)}, u32[]{:S(2)}) %copy-start.6) | copy-done | bytes 524312
  51.7 3.5 %shard_map.146 = (f32[1040,512]{1,0:T(8,128)S(1)}, bf16[1040,512]{1,0:T(8,128)(2,1)S(1)}, bf16[1024,256]{1,0:T(8,128)(2,1)S(1)}, bf16[128,256]{1,0:T(8,128)(2,1)...) custom-call(s32[8,128]{1,0:T(8,128)S(1)} %bitcast.13, bf16[128,512]{1,0:T(8,128)(2,1)S(1)} %copy-done.1, ...), custom_call_target="tpu_custom_call" | custom-call | flops 1835008000 | bytes 3670016 | tf_op jit(solution)/shard_map/pallas_call | solution.py:296
  55.3 0.0 collective-permute-done.2.col_first_ref
  55.3 0.0 collective-permute-done.3.col_second_ref
  55.3 5.6 %shard_map.147 = bf16[128,512]{1,0:T(8,128)(2,1)} custom-call(s32[1]{0:T(128)S(6)} %copy.19.row_ref, s32[2]{0:T(128)S(1)} %pad_add_fusion.odd_ref, f32[1040,512]{1,0:T(8,128)S(1)} %get-tuple-element.18.pre_ref, bf16[1040,512]{1,0:T(8,128)(2,1)S(1)} %get-tuple-element.19.far_ref, bf16[1024,256]{1,0:T(8,128)(2,1)S(1)} %get-tuple-element.20.near_ref, ...), custom_call_target="tpu_custom_call" | custom-call | flops 2621440000 | bytes 5242880 | tf_op jit(solution)/shard_map/pallas_call | solution.py:312
  (27 shorter events, 0.1 us)
Async XLA Ops:
  0.0 50.6 %copy-start.12 = (s32[1024]{0:T(1024)S(1)}, s32[1024]{0:T(1024)}, u32[]{:S(2)}) copy-start(s32[1024]{0:T(1024)} %param.17) | copy-start | bytes 12292
  0.0 50.6 %copy-start.13 = (s32[128]{0:T(128)S(1)}, s32[128]{0:T(128)}, u32[]{:S(2)}) copy-start(s32[128]{0:T(128)} %param.18) | copy-start | bytes 1540
  0.0 50.6 %copy-start.11 = (bf16[16,512]{1,0:T(8,128)(2,1)S(1)}, bf16[16,512]{1,0:T(8,128)(2,1)}, u32[]{:S(2)}) copy-start(bf16[16,512]{1,0:T(8,128)(2,1)} %cedges_ref.1) | copy-start | bytes 49156
  0.8 0.9 %copy-start = (bf16[128,512]{1,0:T(8,128)(2,1)S(1)}, bf16[128,512]{1,0:T(8,128)(2,1)}, u32[]{:S(2)}) copy-start(bf16[128,512]{1,0:T(8,128)(2,1)} %nodes_ref.3) | copy-start | bytes 393220
  1.7 0.7 %copy-start.2 = (s32[128]{0:T(128)S(1)}, s32[128]{0:T(128)}, u32[]{:S(2)}) copy-start(s32[128]{0:T(128)} %param.19) | copy-start | bytes 1540
  2.3 48.3 %copy-start.1 = (bf16[128,512]{1,0:T(8,128)(2,1)S(1)}, bf16[128,512]{1,0:T(8,128)(2,1)}, u32[]{:S(2)}) copy-start(bf16[128,512]{1,0:T(8,128)(2,1)} %nodes_ref.3) | copy-start | bytes 393220
  2.3 48.3 %copy-start.3 = (bf16[1024,512]{1,0:T(8,128)(2,1)S(1)}, bf16[1024,512]{1,0:T(8,128)(2,1)}, u32[]{:S(2)}) copy-start(bf16[1024,512]{1,0:T(8,128)(2,1)} %refs_4_.1) | copy-start | bytes 3145732
  2.3 48.3 %copy-start.4 = (bf16[512,512]{1,0:T(8,128)(2,1)S(1)}, bf16[512,512]{1,0:T(8,128)(2,1)}, u32[]{:S(2)}) copy-start(bf16[512,512]{1,0:T(8,128)(2,1)} %refs_2_.1) | copy-start | bytes 1572868
  2.3 48.3 %copy-start.5 = (bf16[512,512]{1,0:T(8,128)(2,1)S(1)}, bf16[512,512]{1,0:T(8,128)(2,1)}, u32[]{:S(2)}) copy-start(bf16[512,512]{1,0:T(8,128)(2,1)} %refs_3_.1) | copy-start | bytes 1572868
  3.8 27.1 %all-to-all-start = ((bf16[32,4,128]{2,1,0:T(4,128)(2,1)}), bf16[32,4,128]{2,1,0:T(4,128)(2,1)S(1)}, u32[]{:S(2)}, u32[]{:S(2)}) async-start(bf16[32,4,128]{2,1,0:T(4,128)(2,1)} %get-tuple-element.16), calls=%async_computation | async-start | bytes 65536 | tf_op jit(solution)/shard_map/all_to_all | solution.py:270
  19.1 19.7 %collective-permute-start = (bf16[48,512]{1,0:T(8,128)(2,1)S(1)}, bf16[48,512]{1,0:T(8,128)(2,1)S(1)}, u32[]{:S(2)}, u32[]{:S(2)}) collective-permute-start(bf16[48,512]{1,0:T(8,128)(2,1)S(1)} %get-tuple-element.24), channel_id=1, source_target_pairs={{0,16},{1,17},{2,18},{3,19},{4,20},{5,21},{6,22},{7,23},{8,24},{9,... | collective-permute-start | bytes 147464 | tf_op jit(solution)/shard_map/ppermute | solution.py:271
  21.2 17.6 %collective-permute-start.1 = (bf16[48,512]{1,0:T(8,128)(2,1)S(1)}, bf16[48,512]{1,0:T(8,128)(2,1)S(1)}, u32[]{:S(2)}, u32[]{:S(2)}) collective-permute-start(bf16[48,512]{1,0:T(8,128)(2,1)S(1)} %get-tuple-element.25), channel_id=1, source_target_pairs={{0,496},{1,497},{2,498},{3,499},{4,500},{5,501},{6,502},{7,503},{8... | collective-permute-start | bytes 147464 | tf_op jit(solution)/shard_map/ppermute | solution.py:272
  31.8 18.8 %all-to-all-start.1 = ((bf16[16,32,512]{2,1,0:T(8,128)(2,1)}), bf16[16,32,512]{2,1,0:T(8,128)(2,1)S(1)}, u32[]{:S(2)}, u32[]{:S(2)}) async-start(bf16[16,32,512]{2,1,0:T(8,128)(2,1)} %broadcast_in_dim.8), calls=%async_computation.1 | async-start | bytes 1048576 | tf_op jit(solution)/shard_map/all_to_all | solution.py:280
  38.9 16.4 %collective-permute-start.2 = (bf16[48,512]{1,0:T(8,128)(2,1)S(1)}, bf16[48,512]{1,0:T(8,128)(2,1)S(1)}, u32[]{:S(2)}, u32[]{:S(2)}) collective-permute-start(bf16[48,512]{1,0:T(8,128)(2,1)S(1)} %get-tuple-element.28), channel_id=1, source_target_pairs={{0,1},{1,0},{2,3},{3,2},{4,5},{5,4},{6,7},{7,6},{8,9},{9,8},{10,11... | collective-permute-start | bytes 147464 | tf_op jit(solution)/shard_map/ppermute | solution.py:277
  42.4 12.9 %collective-permute-start.3 = (bf16[48,512]{1,0:T(8,128)(2,1)S(1)}, bf16[48,512]{1,0:T(8,128)(2,1)S(1)}, u32[]{:S(2)}, u32[]{:S(2)}) collective-permute-start(bf16[48,512]{1,0:T(8,128)(2,1)S(1)} %get-tuple-element.27), channel_id=1, source_target_pairs={{0,15},{1,2},{2,1},{3,4},{4,3},{5,6},{6,5},{7,8},{8,7},{9,10},{10,... | collective-permute-start | bytes 147464 | tf_op jit(solution)/shard_map/ppermute | solution.py:278
  50.7 1.0 %copy-start.6 = (bf16[512,512]{1,0:T(8,128)(2,1)S(1)}, bf16[512,512]{1,0:T(8,128)(2,1)}, u32[]{:S(2)}) copy-start(bf16[512,512]{1,0:T(8,128)(2,1)} %refs_10_.1) | copy-start | bytes 1572868
  51.7 3.6 %copy-start.7 = (bf16[512,512]{1,0:T(8,128)(2,1)S(1)}, bf16[512,512]{1,0:T(8,128)(2,1)}, u32[]{:S(2)}) copy-start(bf16[512,512]{1,0:T(8,128)(2,1)} %w_sender_ref.1) | copy-start | bytes 1572868
  51.7 3.6 %copy-start.8 = (bf16[512,512]{1,0:T(8,128)(2,1)S(1)}, bf16[512,512]{1,0:T(8,128)(2,1)}, u32[]{:S(2)}) copy-start(bf16[512,512]{1,0:T(8,128)(2,1)} %w_message_ref.1) | copy-start | bytes 1572868
  51.7 3.6 %copy-start.9 = (bf16[512,512]{1,0:T(8,128)(2,1)S(1)}, bf16[512,512]{1,0:T(8,128)(2,1)}, u32[]{:S(2)}) copy-start(bf16[512,512]{1,0:T(8,128)(2,1)} %w_gather_ref.1) | copy-start | bytes 1572868
  51.7 3.6 %copy-start.10 = (bf16[512,512]{1,0:T(8,128)(2,1)S(1)}, bf16[512,512]{1,0:T(8,128)(2,1)}, u32[]{:S(2)}) copy-start(bf16[512,512]{1,0:T(8,128)(2,1)} %w_node_out_ref.1) | copy-start | bytes 1572868

commit v3 on v2

v3 whole, which is shorter than its diff:
```python
import functools

import jax
import jax.numpy as jnp
from jax import lax
from jax.experimental import pallas as pl
from jax.experimental.pallas import tpu as pltpu
from jax.sharding import Mesh
from jax.sharding import PartitionSpec as P

epsilon = 1e-05
AXES = ("y", "zh", "core", "x", "zl")
SIZES = (4, 4, 2, 4, 4)
NEAR = ("zh", "core", "zl")
FAR = ("y", "x")
BF = jnp.bfloat16
F32 = jnp.float32
BLOCK = 256


def dot(a, b):
    return jnp.dot(a, b, preferred_element_type=F32)


def column(row):
    return jnp.transpose(jnp.broadcast_to(row, (128, 128)))


def silu(x):
    half = 0.5 * x
    return half + half * jnp.tanh(half)


def layer_norm(values):
    centred = values - jnp.mean(values, axis=-1, keepdims=True)
    second = jnp.mean(centred * centred, axis=-1, keepdims=True)
    return centred * lax.rsqrt(second + epsilon)


def pick_kernel(
    row_ref, send_ref, nodes_ref, first_ref, second_ref, side_ref, own_ref, message_ref
):
    lanes = lax.broadcasted_iota(jnp.int32, (128, 128), 1)
    chosen = (column(send_ref[...]) == lanes).astype(F32).astype(BF)
    picked = dot(chosen, nodes_ref[...])
    odd = lax.axis_index("core") == 1
    first_ref[...] = jnp.where(odd, picked[0:48, :], picked[80:128, :]).astype(BF)
    second_ref[...] = jnp.where(odd, picked[80:128, :], picked[0:48, :]).astype(BF)
    side_ref[...] = picked[48:80, :].astype(BF)
    chosen = (lanes[:16] == row_ref[0]).astype(F32).astype(BF)
    own = dot(chosen, nodes_ref[...])
    own_ref[...] = own.astype(BF)
    rows = jnp.concatenate([own[0:1, 128 * k : 128 * k + 128] for k in range(4)], axis=0)
    message_ref[...] = jnp.broadcast_to(rows.astype(BF)[None], (32, 4, 128))


def onehot(ids, width):
    lanes = lax.broadcasted_iota(jnp.int32, ids.shape, 1)
    parts = [(ids == lanes + 128 * k).astype(F32).astype(BF) for k in range(width // 128)]
    return jnp.concatenate(parts, axis=1)


def place(c):
    return (c & 0x180) | ((c & 0xC) << 3) | ((c & 0x70) >> 2) | (c & 3)


def local_kernel(
    senders_ref,
    csenders_ref,
    degrees_ref,
    own_ref,
    nodes_ref,
    edges_ref,
    cedges_ref,
    coarse_ref,
    w_edge_ref,
    w_receiver_ref,
    pre_ref,
    far_ref,
    near_ref,
    use_ref,
    agg_ref,
):
    nodes = nodes_ref[...]
    receiver = dot(nodes, w_receiver_ref[...])
    senders = senders_ref[...]
    spots = jnp.where(senders < 256, -1, place(senders - 256))
    wide = lax.broadcasted_iota(jnp.int32, (32, BLOCK), 1)
    node = lax.broadcasted_iota(jnp.int32, (32, BLOCK), 0)
    for b in range(4):
        rows = slice(BLOCK * b, BLOCK * b + BLOCK)
        before = dot(edges_ref[rows, :], w_edge_ref[...])
        own = receiver[32 * b : 32 * b + 32, :]
        pre_ref[rows, :] = before + jnp.broadcast_to(own[:, None, :], (32, 8, 512)).reshape(BLOCK, 512)
    degrees = column(degrees_ref[...])
    for b in range(4):
        rows = slice(BLOCK * b, BLOCK * b + BLOCK)
        ids = [column(senders[2 * b + i : 2 * b + i + 1, :]) for i in range(2)]
        near_ref[rows, :] = onehot(jnp.concatenate(ids, axis=0), 256)
        ids = [column(spots[2 * b + i : 2 * b + i + 1, :]) for i in range(2)]
        chosen = onehot(jnp.concatenate(ids, axis=0), 512)
        far_ref[rows, :] = dot(chosen, coarse_ref[...]).astype(BF)
        deg = degrees[32 * b : 32 * b + 32, :]
        deg = jnp.concatenate([deg, deg], axis=1)
        used = (((wide >> 3) == node) & ((wide & 7) < deg)).astype(F32).astype(BF)
        use_ref[32 * b : 32 * b + 32, :] = used
        agg_ref[32 * b : 32 * b + 32, :] = dot(used, edges_ref[rows, :])
    coarse = dot(cedges_ref[...], w_edge_ref[...])
    pre_ref[1024:1040, :] = coarse + dot(own_ref[...], w_receiver_ref[...])
    chosen = onehot(column(place(csenders_ref[...]))[:16], 512)
    far_ref[1024:1040, :] = dot(chosen, coarse_ref[...]).astype(BF)


def final_kernel(
    row_ref,
    pre_ref,
    far_ref,
    near_ref,
    use_ref,
    agg_ref,
    nodes_ref,
    cedges_ref,
    row_first_ref,
    row_second_ref,
    col_first_ref,
    col_second_ref,
    w_sender_ref,
    w_message_ref,
    w_node_ref,
    w_gather_ref,
    w_node_out_ref,
    out_ref,
    table,
    summed_ref,
):
    odd_row = lax.axis_index("core") == 1
    odd_col = lax.axis_index("zl") % 2 == 1
    table[0:128, :] = nodes_ref[...]
    above = jnp.where(odd_row, row_first_ref[...], row_second_ref[...])
    below = jnp.where(odd_row, row_second_ref[...], row_first_ref[...])
    left = jnp.where(odd_col, col_first_ref[...], col_second_ref[...])
    right = jnp.where(odd_col, col_second_ref[...], col_first_ref[...])
    table[128:144, :] = left[0:16]
    table[144:160, :] = above[16:32]
    table[160:176, :] = right[0:16]
    table[176:192, :] = left[16:32]
    table[192:208, :] = right[16:32]
    table[208:224, :] = left[32:48]
    table[224:240, :] = below[16:32]
    table[240:256, :] = right[32:48]
    node_pre = dot(nodes_ref[...], w_node_ref[...])
    partial = None
    for b in range(4):
        rows = slice(BLOCK * b, BLOCK * b + BLOCK)
        sender = dot(near_ref[rows, :], table[...]).astype(BF) + far_ref[rows, :]
        if b == 3:
            rows = slice(BLOCK * b, BLOCK * b + BLOCK + 16)
            sender = jnp.concatenate([sender, far_ref[1024:1040, :]], axis=0)
        before = pre_ref[rows, :] + dot(sender, w_sender_ref[...])
        hidden = silu(before).astype(BF)
        message = layer_norm(dot(hidden, w_message_ref[...]))
        used = use_ref[32 * b : 32 * b + 32, :]
        high = message[:BLOCK].astype(BF)
        low = (message[:BLOCK] - high.astype(F32)).astype(BF)
        summed_ref[32 * b : 32 * b + 32, :] = (
            agg_ref[32 * b : 32 * b + 32, :] + dot(used, high) + dot(used, low)
        )
        if b == 3:
            updated = cedges_ref[...].astype(F32) + message[BLOCK:]
            partial = jnp.sum(updated, axis=0, keepdims=True)
    owner = lax.broadcasted_iota(jnp.int32, (128, 1), 0) == row_ref[0]
    summed = summed_ref[...] + jnp.where(owner, partial, jnp.zeros_like(partial))
    hidden = silu(node_pre + dot(summed.astype(BF), w_gather_ref[...])).astype(BF)
    result = nodes_ref[...].astype(F32) + layer_norm(dot(hidden, w_node_out_ref[...]))
    out_ref[...] = result.astype(BF)


VMEM = pl.BlockSpec(memory_space=pltpu.VMEM)
SMEM = pl.BlockSpec(memory_space=pltpu.SMEM)


def call(kernel, ins, outs, cost, scratch=(), limit=8):
    return pl.pallas_call(
        kernel,
        in_specs=ins,
        out_specs=[VMEM] * len(outs),
        out_shape=[jax.ShapeDtypeStruct(*o) for o in outs],
        scratch_shapes=scratch,
        cost_estimate=pl.CostEstimate(flops=cost, bytes_accessed=cost // 500, transcendentals=0),
        compiler_params=pltpu.CompilerParams(vmem_limit_bytes=limit * 2**20),
    )


def swap(axis, odd):
    pairs = []
    for flat in range(512):
        at = list(divmod(flat, 16))
        step = 1 if at[axis] % 2 == odd else -1
        at[axis] = (at[axis] + step) % (32, 16)[axis]
        pairs.append((flat, at[0] * 16 + at[1]))
    return pairs


def body(
    node_latents,
    fine_edges,
    fine_senders,
    degrees,
    send_list,
    coarse_row,
    coarse_edges,
    coarse_senders,
    w_edge,
    w_sender,
    w_receiver,
    w_message,
    w_node,
    w_gather,
    w_node_out,
):
    odd_row = lax.axis_index("core") == 1
    odd_col = lax.axis_index("zl") % 2 == 1
    first, second, side, own, message = call(
        pick_kernel,
        [SMEM, VMEM, VMEM],
        [
            ((48, 512), BF),
            ((48, 512), BF),
            ((32, 512), BF),
            ((16, 512), BF),
            ((32, 4, 128), BF),
        ],
        2 * 144 * 128 * 512,
    )(coarse_row, send_list.reshape(1, 128), node_latents)
    z_rows = lax.all_to_all(message, NEAR, 0, 0)
    row_first = lax.ppermute(first, AXES, swap(0, 0))
    row_second = lax.ppermute(second, AXES, swap(0, 1))
    above = jnp.where(odd_row, row_first, row_second)
    below = jnp.where(odd_row, row_second, row_first)
    right = jnp.concatenate([above[32:], side[16:], below[32:]], axis=0)
    left = jnp.concatenate([above[:16], side[:16], below[:16]], axis=0)
    col_first = lax.ppermute(jnp.where(odd_col, left, right), AXES, swap(1, 0))
    col_second = lax.ppermute(jnp.where(odd_col, right, left), AXES, swap(1, 1))
    z_rows = z_rows.reshape(1, 32, 512)
    coarse = lax.all_to_all(jnp.broadcast_to(z_rows, (16, 32, 512)), FAR, 0, 0).reshape(512, 512)
    csenders = jnp.pad(coarse_senders.reshape(1, 16), ((0, 0), (0, 112)))
    pre, far, near, use, agg = call(
        local_kernel,
        [VMEM] * 10,
        [
            ((1040, 512), F32),
            ((1040, 512), BF),
            ((1024, 256), BF),
            ((128, BLOCK), BF),
            ((128, 512), F32),
        ],
        2 * 3500 * 512 * 512,
    )(
        fine_senders.reshape(8, 128),
        csenders,
        degrees.reshape(1, 128),
        own,
        node_latents,
        fine_edges,
        coarse_edges,
        coarse,
        w_edge,
        w_receiver,
    )
    (out,) = call(
        final_kernel,
        [SMEM] + [VMEM] * 16,
        [((128, 512), BF)],
        2 * 5000 * 512 * 512,
        [pltpu.VMEM((256, 512), BF), pltpu.VMEM((128, 512), F32)],
    )(
        coarse_row,
        pre,
        far,
        near,
        use,
        agg,
        node_latents,
        coarse_edges,
        row_first,
        row_second,
        col_first,
        col_second,
        w_sender,
        w_message,
        w_node,
        w_gather,
        w_node_out,
    )
    return out


def solution(mesh):
    fine = Mesh(mesh.devices.reshape(SIZES), AXES)
    rows, lists = P(AXES, None), P(AXES)
    placed = (rows, rows, lists, lists, lists, lists, rows, lists) + (P(),) * 7
    return jax.shard_map(body, mesh=fine, in_specs=placed, out_specs=rows, check_vma=False)
```

time: 61.4 us -> 57.9 us (0.943)
  the two profiles are of different devices: /device:TPU:32 before, /device:TPU:8 now
where the time goes in v3:
time: 57.9 us; the launch traced here: 57.5 us
  starting transfers between devices  40.1 us (69%)
  Pallas kernels  7.7 us (13%)
  waiting for transfers between devices  5.61 us (10%)
  local copies, waits for them, and re-layouts  3.16 us (5%)
  between operations  0.89 us (2%)
    all_to_all x1, starting transfers between devices, body(): z_rows = lax.all_to_all(message, NEAR, 0, 0)  15.5 us
    all_to_all x1, starting transfers between devices, body(): lax.all_to_all(jnp.broadcast_to(z_rows, (16, 32, 512)), FAR, 0, 0)  7.4 us
    ppermute x1, starting transfers between devices, body(): row_second = lax.ppermute(second, AXES, swap(0, 1))  7.38 us
    ppermute x1, starting transfers between devices, body(): col_second = lax.ppermute(jnp.where(odd_col, right, left), AXES, swap(1, 1))  5.24 us
    pallas_call x1, Pallas kernels, body(): call(final_kernel, [SMEM] + [VMEM] * 16, [((128, 512), BF)], 2 * 5000 * 5...  5.1 us
    all_to_all x1, waiting for transfers between devices, body(): z_rows = lax.all_to_all(message, NEAR, 0, 0)  2.81 us
    ppermute x1, starting transfers between devices, body(): col_first = lax.ppermute(jnp.where(odd_col, left, right), AXES, swap(1, 0))  2.41 us
    ppermute x1, starting transfers between devices, body(): row_first = lax.ppermute(first, AXES, swap(0, 0))  2.18 us
  transfers between devices with their start and end apart: 6, of which 3 were waited for; matrix products, arithmetic and copies ran while one was open for 3% of the time, Pallas kernels for 3%

profile of v3, /device:TPU:8, one launch (start us, length us, event | category | flops | bytes accessed | tf_op | source)
XLA Modules:
  0.0 57.5 jit_solution(17417352435579899081)
XLA Ops:
  0.7 0.9 %copy-done = bf16[128,512]{1,0:T(8,128)(2,1)S(1)} copy-done((bf16[128,512]{1,0:T(8,128)(2,1)S(1)}, bf16[128,512]{1,0:T(8,128)(2,1)}, u32[]{:S(2)}) %copy-start) | copy-done | bytes 131096
  1.6 0.7 %copy-done.2 = s32[128]{0:T(128)S(1)} copy-done((s32[128]{0:T(128)S(1)}, s32[128]{0:T(128)}, u32[]{:S(2)}) %copy-start.2) | copy-done | bytes 536
  2.3 0.9 %shard_map.145 = (bf16[48,512]{1,0:T(8,128)(2,1)S(1)}, bf16[48,512]{1,0:T(8,128)(2,1)S(1)}, bf16[32,512]{1,0:T(8,128)(2,1)S(1)}, bf16[16,512]{1,0:T(8,128)(2,1)S(1)}, bf16[32,4,128]{2,1,0:T(4,128)(2,1)}) custom-call(s32[1]{0:T(128)S(6)} %copy.19.row_ref, s32[1,128]{1,0:T(1,128)S(1)} %bitcast.10, bf16[128,512]{1,0:T(8,128)(2,1)S(1)} %copy-done), custom_call_target="tpu_custom_call" | custom-call | flops 18874368 | bytes 37748 | tf_op jit(solution)/shard_map/pallas_call | solution.py:223
  3.1 15.5 %all-to-all-start = ((bf16[32,4,128]{2,1,0:T(4,128)(2,1)}), bf16[32,4,128]{2,1,0:T(4,128)(2,1)S(1)}, u32[]{:S(2)}, u32[]{:S(2)}) async-start(bf16[32,4,128]{2,1,0:T(4,128)(2,1)} %get-tuple-element.16), calls=%async_computation | async-start | bytes 65536 | tf_op jit(solution)/shard_map/all_to_all | solution.py:235
  18.6 2.2 %collective-permute-start = (bf16[48,512]{1,0:T(8,128)(2,1)S(1)}, bf16[48,512]{1,0:T(8,128)(2,1)S(1)}, u32[]{:S(2)}, u32[]{:S(2)}) collective-permute-start(bf16[48,512]{1,0:T(8,128)(2,1)S(1)} %get-tuple-element.22), channel_id=1, source_target_pairs={{0,16},{1,17},{2,18},{3,19},{4,20},{5,21},{6,22},{7,23},{8,24},{9,... | collective-permute-start | bytes 147464 | tf_op jit(solution)/shard_map/ppermute | solution.py:236
  20.8 7.4 %collective-permute-start.1 = (bf16[48,512]{1,0:T(8,128)(2,1)S(1)}, bf16[48,512]{1,0:T(8,128)(2,1)S(1)}, u32[]{:S(2)}, u32[]{:S(2)}) collective-permute-start(bf16[48,512]{1,0:T(8,128)(2,1)S(1)} %get-tuple-element.23), channel_id=1, source_target_pairs={{0,496},{1,497},{2,498},{3,499},{4,500},{5,501},{6,502},{7,503},{8... | collective-permute-start | bytes 147464 | tf_op jit(solution)/shard_map/ppermute | solution.py:237
  28.2 0.7 %pad.4.csenders_ref = s32[1,128]{1,0:T(1,128)S(1)} pad(s32[1,16]{1,0:T(1,128)} %bitcast.15, s32[]{:T(128)} %constant.19.clone.1), padding=0_0x0_112 | pad | bytes 580 | tf_op jit(solution)/shard_map/jit(_pad)/pad | solution.py:246
  28.9 2.8 %all-to-all-done = bf16[32,4,128]{2,1,0:T(4,128)(2,1)S(1)} async-done(((bf16[32,4,128]{2,1,0:T(4,128)(2,1)}), bf16[32,4,128]{2,1,0:T(4,128)(2,1)S(1)}, u32[]{:S(2)}, u32[]{:S(2)}) %all-to-all-start) | async-done | bytes 32800 | tf_op jit(solution)/shard_map/all_to_all | solution.py:235
  31.7 0.9 %broadcast_in_dim.8 = bf16[16,32,512]{2,1,0:T(8,128)(2,1)} broadcast(bf16[32,512]{1,0:T(8,128)(2,1)S(1)} %bitcast.13), dimensions={1,2} | broadcast | bytes 557056 | tf_op jit(solution)/shard_map/broadcast_in_dim | solution.py:245
  32.6 7.4 %all-to-all-start.1 = ((bf16[16,32,512]{2,1,0:T(8,128)(2,1)}), bf16[16,32,512]{2,1,0:T(8,128)(2,1)S(1)}, u32[]{:S(2)}, u32[]{:S(2)}) async-start(bf16[16,32,512]{2,1,0:T(8,128)(2,1)} %broadcast_in_dim.8), calls=%async_computation.1 | async-start | bytes 1048576 | tf_op jit(solution)/shard_map/all_to_all | solution.py:245
  40.0 0.0 collective-permute-done.row_first_ref
  40.0 0.0 collective-permute-done.1.row_second_ref
  40.0 2.4 %collective-permute-start.2 = (bf16[48,512]{1,0:T(8,128)(2,1)S(1)}, bf16[48,512]{1,0:T(8,128)(2,1)S(1)}, u32[]{:S(2)}, u32[]{:S(2)}) collective-permute-start(bf16[48,512]{1,0:T(8,128)(2,1)S(1)} %get-tuple-element.26), channel_id=1, source_target_pairs={{0,1},{1,0},{2,3},{3,2},{4,5},{5,4},{6,7},{7,6},{8,9},{9,8},{10,11... | collective-permute-start | bytes 147464 | tf_op jit(solution)/shard_map/ppermute | solution.py:242
  42.5 5.2 %collective-permute-start.3 = (bf16[48,512]{1,0:T(8,128)(2,1)S(1)}, bf16[48,512]{1,0:T(8,128)(2,1)S(1)}, u32[]{:S(2)}, u32[]{:S(2)}) collective-permute-start(bf16[48,512]{1,0:T(8,128)(2,1)S(1)} %get-tuple-element.25), channel_id=1, source_target_pairs={{0,15},{1,2},{2,1},{3,4},{4,3},{5,6},{6,5},{7,8},{8,7},{9,10},{10,... | collective-permute-start | bytes 147464 | tf_op jit(solution)/shard_map/ppermute | solution.py:243
  47.7 0.9 %all-to-all-done.1 = bf16[16,32,512]{2,1,0:T(8,128)(2,1)S(1)} async-done(((bf16[16,32,512]{2,1,0:T(8,128)(2,1)}), bf16[16,32,512]{2,1,0:T(8,128)(2,1)S(1)}, u32[]{:S(2)}, u32[]{:S(2)}) %all-to-all-start.1) | async-done | bytes 524320 | tf_op jit(solution)/shard_map/all_to_all | solution.py:245
  48.7 0.0 copy-start.6
  48.7 0.0 copy-start.7
  48.7 0.0 copy-start.8
  48.7 0.0 copy-start.9
  48.7 0.0 copy-start.10
  48.7 1.7 %shard_map.146 = (f32[1040,512]{1,0:T(8,128)S(1)}, bf16[1040,512]{1,0:T(8,128)(2,1)S(1)}, bf16[1024,256]{1,0:T(8,128)(2,1)S(1)}, bf16[128,256]{1,0:T(8,128)(2,1)S(1)}, f32[128,512]{1,0:T(8,128)S(1)}) custom-call(s32[8,128]{1,0:T(8,128)S(1)} %bitcast.11, s32[1,128]{1,0:T(1,128)S(1)} %pad.4.csenders_ref, s32[1,128]{1,0:T(1,128)S(1)} %bitcast.12, ...), custom_call_target="tpu_custom_call" | custom-call | flops 1835008000 | bytes 3670016 | tf_op jit(solution)/shard_map/pallas_call | solution.py:247
  50.5 0.0 collective-permute-done.2.col_first_ref
  50.5 1.9 %collective-permute-done.3.col_second_ref = bf16[48,512]{1,0:T(8,128)(2,1)S(1)} collective-permute-done((bf16[48,512]{1,0:T(8,128)(2,1)S(1)}, bf16[48,512]{1,0:T(8,128)(2,1)S(1)}, u32[]{:S(2)}, u32[]{:S(2)}) %collective-permute-start.3) | collective-permute-done | bytes 49184 | tf_op jit(solution)/shard_map/ppermute | solution.py:243
  52.4 5.1 %shard_map.147 = bf16[128,512]{1,0:T(8,128)(2,1)} custom-call(s32[1]{0:T(128)S(6)} %copy.19.row_ref, f32[1040,512]{1,0:T(8,128)S(1)} %get-tuple-element.17.pre_ref, bf16[1040,512]{1,0:T(8,128)(2,1)S(1)} %get-tuple-element.18.far_ref, bf16[1024,256]{1,0:T(8,128)(2,1)S(1)} %get-tuple-element.19.near_ref, bf16[128,256]{1,0:T(8,128)(2,1)S(1)} %get-tuple-element.20.use_ref, ...), custom_call_target="tpu_custom_call" | custom-call | flops 2621440000 | bytes 5242880 | tf_op jit(solution)/shard_map/pallas_call | solution.py:270
  (26 shorter events, 0.1 us)
Async XLA Ops:
  0.0 48.6 %copy-start.13 = (s32[128]{0:T(128)S(1)}, s32[128]{0:T(128)}, u32[]{:S(2)}) copy-start(s32[128]{0:T(128)} %param.18) | copy-start | bytes 1540
  0.7 0.9 %copy-start = (bf16[128,512]{1,0:T(8,128)(2,1)S(1)}, bf16[128,512]{1,0:T(8,128)(2,1)}, u32[]{:S(2)}) copy-start(bf16[128,512]{1,0:T(8,128)(2,1)} %nodes_ref.5) | copy-start | bytes 393220
  1.6 0.7 %copy-start.2 = (s32[128]{0:T(128)S(1)}, s32[128]{0:T(128)}, u32[]{:S(2)}) copy-start(s32[128]{0:T(128)} %param.19) | copy-start | bytes 1540
  2.2 46.4 %copy-start.1 = (bf16[128,512]{1,0:T(8,128)(2,1)S(1)}, bf16[128,512]{1,0:T(8,128)(2,1)}, u32[]{:S(2)}) copy-start(bf16[128,512]{1,0:T(8,128)(2,1)} %nodes_ref.5) | copy-start | bytes 393220
  2.2 46.4 %copy-start.3 = (bf16[1024,512]{1,0:T(8,128)(2,1)S(1)}, bf16[1024,512]{1,0:T(8,128)(2,1)}, u32[]{:S(2)}) copy-start(bf16[1024,512]{1,0:T(8,128)(2,1)} %edges_ref.1) | copy-start | bytes 3145732
  2.2 46.4 %copy-start.4 = (bf16[512,512]{1,0:T(8,128)(2,1)S(1)}, bf16[512,512]{1,0:T(8,128)(2,1)}, u32[]{:S(2)}) copy-start(bf16[512,512]{1,0:T(8,128)(2,1)} %w_edge_ref.1) | copy-start | bytes 1572868
  2.2 46.4 %copy-start.5 = (bf16[512,512]{1,0:T(8,128)(2,1)S(1)}, bf16[512,512]{1,0:T(8,128)(2,1)}, u32[]{:S(2)}) copy-start(bf16[512,512]{1,0:T(8,128)(2,1)} %w_receiver_ref.1) | copy-start | bytes 1572868
  2.2 46.4 %copy-start.11 = (bf16[16,512]{1,0:T(8,128)(2,1)S(1)}, bf16[16,512]{1,0:T(8,128)(2,1)}, u32[]{:S(2)}) copy-start(bf16[16,512]{1,0:T(8,128)(2,1)} %cedges_ref.3) | copy-start | bytes 49156
  2.3 46.4 %copy-start.12 = (s32[1024]{0:T(1024)S(1)}, s32[1024]{0:T(1024)}, u32[]{:S(2)}) copy-start(s32[1024]{0:T(1024)} %param.17) | copy-start | bytes 12292
  3.1 28.6 %all-to-all-start = ((bf16[32,4,128]{2,1,0:T(4,128)(2,1)}), bf16[32,4,128]{2,1,0:T(4,128)(2,1)S(1)}, u32[]{:S(2)}, u32[]{:S(2)}) async-start(bf16[32,4,128]{2,1,0:T(4,128)(2,1)} %get-tuple-element.16), calls=%async_computation | async-start | bytes 65536 | tf_op jit(solution)/shard_map/all_to_all | solution.py:235
  18.6 21.3 %collective-permute-start = (bf16[48,512]{1,0:T(8,128)(2,1)S(1)}, bf16[48,512]{1,0:T(8,128)(2,1)S(1)}, u32[]{:S(2)}, u32[]{:S(2)}) collective-permute-start(bf16[48,512]{1,0:T(8,128)(2,1)S(1)} %get-tuple-element.22), channel_id=1, source_target_pairs={{0,16},{1,17},{2,18},{3,19},{4,20},{5,21},{6,22},{7,23},{8,24},{9,... | collective-permute-start | bytes 147464 | tf_op jit(solution)/shard_map/ppermute | solution.py:236
  20.8 19.2 %collective-permute-start.1 = (bf16[48,512]{1,0:T(8,128)(2,1)S(1)}, bf16[48,512]{1,0:T(8,128)(2,1)S(1)}, u32[]{:S(2)}, u32[]{:S(2)}) collective-permute-start(bf16[48,512]{1,0:T(8,128)(2,1)S(1)} %get-tuple-element.23), channel_id=1, source_target_pairs={{0,496},{1,497},{2,498},{3,499},{4,500},{5,501},{6,502},{7,503},{8... | collective-permute-start | bytes 147464 | tf_op jit(solution)/shard_map/ppermute | solution.py:237
  32.6 16.1 %all-to-all-start.1 = ((bf16[16,32,512]{2,1,0:T(8,128)(2,1)}), bf16[16,32,512]{2,1,0:T(8,128)(2,1)S(1)}, u32[]{:S(2)}, u32[]{:S(2)}) async-start(bf16[16,32,512]{2,1,0:T(8,128)(2,1)} %broadcast_in_dim.8), calls=%async_computation.1 | async-start | bytes 1048576 | tf_op jit(solution)/shard_map/all_to_all | solution.py:245
  40.0 10.4 %collective-permute-start.2 = (bf16[48,512]{1,0:T(8,128)(2,1)S(1)}, bf16[48,512]{1,0:T(8,128)(2,1)S(1)}, u32[]{:S(2)}, u32[]{:S(2)}) collective-permute-start(bf16[48,512]{1,0:T(8,128)(2,1)S(1)} %get-tuple-element.26), channel_id=1, source_target_pairs={{0,1},{1,0},{2,3},{3,2},{4,5},{5,4},{6,7},{7,6},{8,9},{9,8},{10,11... | collective-permute-start | bytes 147464 | tf_op jit(solution)/shard_map/ppermute | solution.py:242
  42.5 9.9 %collective-permute-start.3 = (bf16[48,512]{1,0:T(8,128)(2,1)S(1)}, bf16[48,512]{1,0:T(8,128)(2,1)S(1)}, u32[]{:S(2)}, u32[]{:S(2)}) collective-permute-start(bf16[48,512]{1,0:T(8,128)(2,1)S(1)} %get-tuple-element.25), channel_id=1, source_target_pairs={{0,15},{1,2},{2,1},{3,4},{4,3},{5,6},{6,5},{7,8},{8,7},{9,10},{10,... | collective-permute-start | bytes 147464 | tf_op jit(solution)/shard_map/ppermute | solution.py:243
  48.7 3.7 %copy-start.6 = (bf16[512,512]{1,0:T(8,128)(2,1)S(1)}, bf16[512,512]{1,0:T(8,128)(2,1)}, u32[]{:S(2)}) copy-start(bf16[512,512]{1,0:T(8,128)(2,1)} %w_sender_ref.1) | copy-start | bytes 1572868
  48.7 3.7 %copy-start.7 = (bf16[512,512]{1,0:T(8,128)(2,1)S(1)}, bf16[512,512]{1,0:T(8,128)(2,1)}, u32[]{:S(2)}) copy-start(bf16[512,512]{1,0:T(8,128)(2,1)} %w_message_ref.1) | copy-start | bytes 1572868
  48.7 3.7 %copy-start.8 = (bf16[512,512]{1,0:T(8,128)(2,1)S(1)}, bf16[512,512]{1,0:T(8,128)(2,1)}, u32[]{:S(2)}) copy-start(bf16[512,512]{1,0:T(8,128)(2,1)} %w_node_ref.1) | copy-start | bytes 1572868
  48.7 3.7 %copy-start.9 = (bf16[512,512]{1,0:T(8,128)(2,1)S(1)}, bf16[512,512]{1,0:T(8,128)(2,1)}, u32[]{:S(2)}) copy-start(bf16[512,512]{1,0:T(8,128)(2,1)} %w_gather_ref.1) | copy-start | bytes 1572868
  48.7 3.7 %copy-start.10 = (bf16[512,512]{1,0:T(8,128)(2,1)S(1)}, bf16[512,512]{1,0:T(8,128)(2,1)}, u32[]{:S(2)}) copy-start(bf16[512,512]{1,0:T(8,128)(2,1)} %w_node_out_ref.1) | copy-start | bytes 1572868

commit v4 on v3

--- a/solution.py
+++ b/solution.py
@@ -38,8 +38,29 @@
 
 
 def pick_kernel(
-    row_ref, send_ref, nodes_ref, first_ref, second_ref, side_ref, own_ref, message_ref
+    row_from,
+    send_from,
+    nodes_from,
+    first_ref,
+    second_ref,
+    side_ref,
+    own_ref,
+    message_ref,
+    row_ref,
+    send_ref,
+    nodes_ref,
+    sems,
 ):
+    copies = [
+        pltpu.make_async_copy(source, target, sems.at[i])
+        for i, (source, target) in enumerate(
+            ((nodes_from, nodes_ref), (send_from, send_ref), (row_from, row_ref))
+        )
+    ]
+    for copy in copies:
+        copy.start()
+    for copy in copies:
+        copy.wait()
     lanes = lax.broadcasted_iota(jnp.int32, (128, 128), 1)
     chosen = (column(send_ref[...]) == lanes).astype(F32).astype(BF)
     picked = dot(chosen, nodes_ref[...])
@@ -107,7 +128,8 @@
         agg_ref[32 * b : 32 * b + 32, :] = dot(used, edges_ref[rows, :])
     coarse = dot(cedges_ref[...], w_edge_ref[...])
     pre_ref[1024:1040, :] = coarse + dot(own_ref[...], w_receiver_ref[...])
-    chosen = onehot(column(place(csenders_ref[...]))[:16], 512)
+    csenders = jnp.concatenate([csenders_ref[...], jnp.zeros((1, 112), jnp.int32)], axis=1)
+    chosen = onehot(column(place(csenders))[:16], 512)
     far_ref[1024:1040, :] = dot(chosen, coarse_ref[...]).astype(BF)
 
 
@@ -150,6 +172,7 @@
     table[240:256, :] = right[32:48]
     node_pre = dot(nodes_ref[...], w_node_ref[...])
     partial = None
+    hiddens = []
     for b in range(4):
         rows = slice(BLOCK * b, BLOCK * b + BLOCK)
         sender = dot(near_ref[rows, :], table[...]).astype(BF) + far_ref[rows, :]
@@ -157,7 +180,9 @@
             rows = slice(BLOCK * b, BLOCK * b + BLOCK + 16)
             sender = jnp.concatenate([sender, far_ref[1024:1040, :]], axis=0)
         before = pre_ref[rows, :] + dot(sender, w_sender_ref[...])
-        hidden = silu(before).astype(BF)
+        hiddens.append(silu(before).astype(BF))
+    for b in range(4):
+        hidden = hiddens[b]
         message = layer_norm(dot(hidden, w_message_ref[...]))
         used = use_ref[32 * b : 32 * b + 32, :]
         high = message[:BLOCK].astype(BF)
@@ -168,7 +193,7 @@
         if b == 3:
             updated = cedges_ref[...].astype(F32) + message[BLOCK:]
             partial = jnp.sum(updated, axis=0, keepdims=True)
-    owner = lax.broadcasted_iota(jnp.int32, (128, 1), 0) == row_ref[0]
+    owner = lax.broadcasted_iota(jnp.int32, (128, 1), 0) == row_ref[...]
     summed = summed_ref[...] + jnp.where(owner, partial, jnp.zeros_like(partial))
     hidden = silu(node_pre + dot(summed.astype(BF), w_gather_ref[...])).astype(BF)
     result = nodes_ref[...].astype(F32) + layer_norm(dot(hidden, w_node_out_ref[...]))
@@ -176,7 +201,7 @@
 
 
 VMEM = pl.BlockSpec(memory_space=pltpu.VMEM)
-SMEM = pl.BlockSpec(memory_space=pltpu.SMEM)
+ANY = pl.BlockSpec(memory_space=pl.ANY)
 
 
 def call(kernel, ins, outs, cost, scratch=(), limit=8):
@@ -222,7 +247,7 @@
     odd_col = lax.axis_index("zl") % 2 == 1
     first, second, side, own, message = call(
         pick_kernel,
-        [SMEM, VMEM, VMEM],
+        [ANY] * 3,
         [
             ((48, 512), BF),
             ((48, 512), BF),
@@ -231,6 +256,13 @@
             ((32, 4, 128), BF),
         ],
         2 * 144 * 128 * 512,
+        [
+            pltpu.SMEM((1,), jnp.int32),
+            pltpu.VMEM((1, 128), jnp.int32),
+            pltpu.VMEM((128, 512), BF),
+            pltpu.SemaphoreType.DMA((3,)),
+        ],
+        limit=56,
     )(coarse_row, send_list.reshape(1, 128), node_latents)
     z_rows = lax.all_to_all(message, NEAR, 0, 0)
     row_first = lax.ppermute(first, AXES, swap(0, 0))
@@ -243,7 +275,6 @@
     col_second = lax.ppermute(jnp.where(odd_col, right, left), AXES, swap(1, 1))
     z_rows = z_rows.reshape(1, 32, 512)
     coarse = lax.all_to_all(jnp.broadcast_to(z_rows, (16, 32, 512)), FAR, 0, 0).reshape(512, 512)
-    csenders = jnp.pad(coarse_senders.reshape(1, 16), ((0, 0), (0, 112)))
     pre, far, near, use, agg = call(
         local_kernel,
         [VMEM] * 10,
@@ -257,7 +288,7 @@
         2 * 3500 * 512 * 512,
     )(
         fine_senders.reshape(8, 128),
-        csenders,
+        coarse_senders.reshape(1, 16),
         degrees.reshape(1, 128),
         own,
         node_latents,
@@ -269,12 +300,12 @@
     )
     (out,) = call(
         final_kernel,
-        [SMEM] + [VMEM] * 16,
+        [VMEM] * 17,
         [((128, 512), BF)],
         2 * 5000 * 512 * 512,
         [pltpu.VMEM((256, 512), BF), pltpu.VMEM((128, 512), F32)],
     )(
-        coarse_row,
+        coarse_row.reshape(1, 1),
         pre,
         far,
         near,

time: 57.9 us -> 57.3 us (0.990)
  local copies, waits for them, and re-layouts: 3.16 us -> 1.69 us
  Pallas kernels: 7.7 us -> 8.35 us
    unnamed x29, local copies, waits for them, and re-layouts: 1.62 us -> 0.07 us
    slice x2, local copies, waits for them, and re-layouts: 0.01 us -> 0.75 us  [body(): left = jnp.concatenate([above[:16], side[:16], below[:16]], axis=0)]
    pad x1 -> x0, local copies, waits for them, and re-layouts: 0.66 us -> none  [body(): csenders = jnp.pad(coarse_senders.reshape(1, 16), ((0, 0), (0, 112)))]
    pallas_call x2, Pallas kernels: 5.97 us -> 6.61 us  [the longest x1 4.79 us: body(): call(final_kernel, [VMEM] * 17, [((128, 512), BF)], 2 * 5000 * 512 * 512,...]
where the time goes in v4:
time: 57.3 us; the launch traced here: 56.8 us
  starting transfers between devices  40.1 us (70%)
  Pallas kernels  8.35 us (15%)
  waiting for transfers between devices  5.55 us (10%)
  local copies, waits for them, and re-layouts  1.69 us (3%)
  between operations  1.05 us (2%)
    all_to_all x1, starting transfers between devices, body(): z_rows = lax.all_to_all(message, NEAR, 0, 0)  15.5 us
    all_to_all x1, starting transfers between devices, body(): lax.all_to_all(jnp.broadcast_to(z_rows, (16, 32, 512)), FAR, 0, 0)  7.42 us
    ppermute x1, starting transfers between devices, body(): row_second = lax.ppermute(second, AXES, swap(0, 1))  7.37 us
    ppermute x1, starting transfers between devices, body(): col_second = lax.ppermute(jnp.where(odd_col, right, left), AXES, swap(1, 1))  5.2 us
    pallas_call x1, Pallas kernels, body(): call(final_kernel, [VMEM] * 17, [((128, 512), BF)], 2 * 5000 * 512 * 512,...  4.79 us
    all_to_all x1, waiting for transfers between devices, body(): z_rows = lax.all_to_all(message, NEAR, 0, 0)  2.72 us
    ppermute x1, starting transfers between devices, body(): col_first = lax.ppermute(jnp.where(odd_col, left, right), AXES, swap(1, 0))  2.45 us
    ppermute x1, starting transfers between devices, body(): row_first = lax.ppermute(first, AXES, swap(0, 0))  2.18 us
  transfers between devices with their start and end apart: 6, of which 3 were waited for; matrix products, arithmetic and copies ran while one was open for 3% of the time, Pallas kernels for 3%

profile of v4, /device:TPU:8, one launch (start us, length us, event | category | flops | bytes accessed | tf_op | source)
XLA Modules:
  0.0 56.8 jit_solution(6570398855256679499)
XLA Ops:
  0.0 0.0 copy-start.13
  0.0 0.0 copy-start.1
  0.9 1.8 %shard_map.145 = (bf16[48,512]{1,0:T(8,128)(2,1)}, bf16[48,512]{1,0:T(8,128)(2,1)}, bf16[32,512]{1,0:T(8,128)(2,1)}, bf16[16,512]{1,0:T(8,128)(2,1)}, bf16[32,4,128]{2,1,0:T(4,128)(2,1)}) custom-call(s32[1]{0:T(128)} %copy.19.row_from, s32[1,128]{1,0:T(1,128)} %bitcast.17, bf16[128,512]{1,0:T(8,128)(2,1)} %nodes_ref.3), custom_call_target="tpu_custom_call" | custom-call | flops 18874368 | bytes 37748 | tf_op jit(solution)/shard_map/pallas_call | solution.py:248
  2.7 15.5 %all-to-all-start = ((bf16[32,4,128]{2,1,0:T(4,128)(2,1)}), bf16[32,4,128]{2,1,0:T(4,128)(2,1)S(1)}, u32[]{:S(2)}, u32[]{:S(2)}) async-start(bf16[32,4,128]{2,1,0:T(4,128)(2,1)} %get-tuple-element.16), calls=%async_computation | async-start | bytes 65536 | tf_op jit(solution)/shard_map/all_to_all | solution.py:267
  18.2 2.2 %collective-permute-start = (bf16[48,512]{1,0:T(8,128)(2,1)}, bf16[48,512]{1,0:T(8,128)(2,1)S(1)}, u32[]{:S(2)}, u32[]{:S(2)}) collective-permute-start(bf16[48,512]{1,0:T(8,128)(2,1)} %get-tuple-element.22), channel_id=1, source_target_pairs={{0,16},{1,17},{2,18},{3,19},{4,20},{5,21},{6,22},{7,23},{8,24},{9,... | collective-permute-start | bytes 147464 | tf_op jit(solution)/shard_map/ppermute | solution.py:268
  20.4 7.4 %collective-permute-start.1 = (bf16[48,512]{1,0:T(8,128)(2,1)}, bf16[48,512]{1,0:T(8,128)(2,1)S(1)}, u32[]{:S(2)}, u32[]{:S(2)}) collective-permute-start(bf16[48,512]{1,0:T(8,128)(2,1)} %get-tuple-element.23), channel_id=1, source_target_pairs={{0,496},{1,497},{2,498},{3,499},{4,500},{5,501},{6,502},{7,503},{8... | collective-permute-start | bytes 147464 | tf_op jit(solution)/shard_map/ppermute | solution.py:269
  27.8 0.7 %fusion.2 = (bf16[16,512]{1,0:T(8,128)(2,1)S(1)}, bf16[16,512]{1,0:T(8,128)(2,1)S(1)}) fusion(bf16[32,512]{1,0:T(8,128)(2,1)} %get-tuple-element.24), kind=kLoop, calls=%fused_computation.9 | loop fusion | bytes 65536 | tf_op jit(solution)/shard_map/slice | solution.py:273
  28.5 2.7 %all-to-all-done = bf16[32,4,128]{2,1,0:T(4,128)(2,1)S(1)} async-done(((bf16[32,4,128]{2,1,0:T(4,128)(2,1)}), bf16[32,4,128]{2,1,0:T(4,128)(2,1)S(1)}, u32[]{:S(2)}, u32[]{:S(2)}) %all-to-all-start) | async-done | bytes 32800 | tf_op jit(solution)/shard_map/all_to_all | solution.py:267
  31.2 0.9 %broadcast_in_dim.8 = bf16[16,32,512]{2,1,0:T(8,128)(2,1)} broadcast(bf16[32,512]{1,0:T(8,128)(2,1)S(1)} %bitcast.15), dimensions={1,2} | broadcast | bytes 557056 | tf_op jit(solution)/shard_map/broadcast_in_dim | solution.py:277
  32.1 7.4 %all-to-all-start.1 = ((bf16[16,32,512]{2,1,0:T(8,128)(2,1)}), bf16[16,32,512]{2,1,0:T(8,128)(2,1)S(1)}, u32[]{:S(2)}, u32[]{:S(2)}) async-start(bf16[16,32,512]{2,1,0:T(8,128)(2,1)} %broadcast_in_dim.8), calls=%async_computation.1 | async-start | bytes 1048576 | tf_op jit(solution)/shard_map/all_to_all | solution.py:277
  39.5 0.0 collective-permute-done.row_first_ref
  39.5 0.0 collective-permute-done.1.row_second_ref
  39.6 2.4 %collective-permute-start.2 = (bf16[48,512]{1,0:T(8,128)(2,1)S(1)}, bf16[48,512]{1,0:T(8,128)(2,1)S(1)}, u32[]{:S(2)}, u32[]{:S(2)}) collective-permute-start(bf16[48,512]{1,0:T(8,128)(2,1)S(1)} %get-tuple-element.26), channel_id=1, source_target_pairs={{0,1},{1,0},{2,3},{3,2},{4,5},{5,4},{6,7},{7,6},{8,9},{9,8},{10,11... | collective-permute-start | bytes 147464 | tf_op jit(solution)/shard_map/ppermute | solution.py:274
  42.1 5.2 %collective-permute-start.3 = (bf16[48,512]{1,0:T(8,128)(2,1)S(1)}, bf16[48,512]{1,0:T(8,128)(2,1)S(1)}, u32[]{:S(2)}, u32[]{:S(2)}) collective-permute-start(bf16[48,512]{1,0:T(8,128)(2,1)S(1)} %get-tuple-element.25), channel_id=1, source_target_pairs={{0,15},{1,2},{2,1},{3,4},{4,3},{5,6},{6,5},{7,8},{8,7},{9,10},{10,... | collective-permute-start | bytes 147464 | tf_op jit(solution)/shard_map/ppermute | solution.py:275
  47.3 0.9 %all-to-all-done.1 = bf16[16,32,512]{2,1,0:T(8,128)(2,1)S(1)} async-done(((bf16[16,32,512]{2,1,0:T(8,128)(2,1)}), bf16[16,32,512]{2,1,0:T(8,128)(2,1)S(1)}, u32[]{:S(2)}, u32[]{:S(2)}) %all-to-all-start.1) | async-done | bytes 524320 | tf_op jit(solution)/shard_map/all_to_all | solution.py:277
  48.3 0.0 copy-start.4
  48.3 0.0 copy-start.5
  48.3 0.0 copy-start.6
  48.3 0.0 copy-start.7
  48.3 0.0 copy-start.8
  48.4 1.7 %shard_map.146 = (f32[1040,512]{1,0:T(8,128)S(1)}, bf16[1040,512]{1,0:T(8,128)(2,1)S(1)}, bf16[1024,256]{1,0:T(8,128)(2,1)S(1)}, bf16[128,256]{1,0:T(8,128)(2,1)S(1)}, f32[128,512]{1,0:T(8,128)S(1)}) custom-call(s32[8,128]{1,0:T(8,128)S(1)} %bitcast.12, s32[1,16]{1,0:T(1,128)S(1)} %bitcast.13, s32[1,128]{1,0:T(1,128)S(1)} %bitcast.14, ...), custom_call_target="tpu_custom_call" | custom-call | flops 1835008000 | bytes 3670016 | tf_op jit(solution)/shard_map/pallas_call | solution.py:278
  50.1 0.0 collective-permute-done.2.col_first_ref
  50.1 1.9 %collective-permute-done.3.col_second_ref = bf16[48,512]{1,0:T(8,128)(2,1)S(1)} collective-permute-done((bf16[48,512]{1,0:T(8,128)(2,1)S(1)}, bf16[48,512]{1,0:T(8,128)(2,1)S(1)}, u32[]{:S(2)}, u32[]{:S(2)}) %collective-permute-start.3) | collective-permute-done | bytes 49184 | tf_op jit(solution)/shard_map/ppermute | solution.py:275
  52.0 4.8 %shard_map.147 = bf16[128,512]{1,0:T(8,128)(2,1)} custom-call(s32[1,1]{1,0:T(1,128)} %bitcast.10.row_ref, f32[1040,512]{1,0:T(8,128)S(1)} %get-tuple-element.17.pre_ref, bf16[1040,512]{1,0:T(8,128)(2,1)S(1)} %get-tuple-element.18.far_ref, bf16[1024,256]{1,0:T(8,128)(2,1)S(1)} %get-tuple-element.19.near_ref, bf16[128,256]{1,0:T(8,128)(2,1)S(1)} %get-tuple-element.20.use_ref, ...), custom_call_target="tpu_custom_call" | custom-call | flops 2621440000 | bytes 5242880 | tf_op jit(solution)/shard_map/pallas_call | solution.py:301
  (25 shorter events, 0.1 us)
Async XLA Ops:
  0.0 48.2 %copy-start = (bf16[128,512]{1,0:T(8,128)(2,1)S(1)}, bf16[128,512]{1,0:T(8,128)(2,1)}, u32[]{:S(2)}) copy-start(bf16[128,512]{1,0:T(8,128)(2,1)} %nodes_ref.3) | copy-start | bytes 393220
  0.0 48.2 %copy-start.11 = (s32[1024]{0:T(1024)S(1)}, s32[1024]{0:T(1024)}, u32[]{:S(2)}) copy-start(s32[1024]{0:T(1024)} %param.17) | copy-start | bytes 12292
  0.0 48.2 %copy-start.12 = (s32[16]{0:T(128)S(1)}, s32[16]{0:T(128)}, u32[]{:S(2)}) copy-start(s32[16]{0:T(128)} %param.22) | copy-start | bytes 196
  0.0 48.2 %copy-start.13 = (s32[128]{0:T(128)S(1)}, s32[128]{0:T(128)}, u32[]{:S(2)}) copy-start(s32[128]{0:T(128)} %param.18) | copy-start | bytes 1540
  0.0 48.2 %copy-start.1 = (bf16[1024,512]{1,0:T(8,128)(2,1)S(1)}, bf16[1024,512]{1,0:T(8,128)(2,1)}, u32[]{:S(2)}) copy-start(bf16[1024,512]{1,0:T(8,128)(2,1)} %edges_ref.1) | copy-start | bytes 3145732
  0.0 48.2 %copy-start.9 = (bf16[16,512]{1,0:T(8,128)(2,1)S(1)}, bf16[16,512]{1,0:T(8,128)(2,1)}, u32[]{:S(2)}) copy-start(bf16[16,512]{1,0:T(8,128)(2,1)} %cedges_ref.3) | copy-start | bytes 49156
  0.0 48.2 %copy-start.2 = (bf16[512,512]{1,0:T(8,128)(2,1)S(1)}, bf16[512,512]{1,0:T(8,128)(2,1)}, u32[]{:S(2)}) copy-start(bf16[512,512]{1,0:T(8,128)(2,1)} %w_edge_ref.1) | copy-start | bytes 1572868
  0.0 48.2 %copy-start.3 = (bf16[512,512]{1,0:T(8,128)(2,1)S(1)}, bf16[512,512]{1,0:T(8,128)(2,1)}, u32[]{:S(2)}) copy-start(bf16[512,512]{1,0:T(8,128)(2,1)} %w_receiver_ref.1) | copy-start | bytes 1572868
  2.7 45.6 %copy-start.10 = (bf16[16,512]{1,0:T(8,128)(2,1)S(1)}, bf16[16,512]{1,0:T(8,128)(2,1)}, u32[]{:S(2)}) copy-start(bf16[16,512]{1,0:T(8,128)(2,1)} %get-tuple-element.15.own_ref) | copy-start | bytes 49156
  2.7 28.5 %all-to-all-start = ((bf16[32,4,128]{2,1,0:T(4,128)(2,1)}), bf16[32,4,128]{2,1,0:T(4,128)(2,1)S(1)}, u32[]{:S(2)}, u32[]{:S(2)}) async-start(bf16[32,4,128]{2,1,0:T(4,128)(2,1)} %get-tuple-element.16), calls=%async_computation | async-start | bytes 65536 | tf_op jit(solution)/shard_map/all_to_all | solution.py:267
  18.2 21.3 %collective-permute-start = (bf16[48,512]{1,0:T(8,128)(2,1)}, bf16[48,512]{1,0:T(8,128)(2,1)S(1)}, u32[]{:S(2)}, u32[]{:S(2)}) collective-permute-start(bf16[48,512]{1,0:T(8,128)(2,1)} %get-tuple-element.22), channel_id=1, source_target_pairs={{0,16},{1,17},{2,18},{3,19},{4,20},{5,21},{6,22},{7,23},{8,24},{9,... | collective-permute-start | bytes 147464 | tf_op jit(solution)/shard_map/ppermute | solution.py:268
  20.4 19.2 %collective-permute-start.1 = (bf16[48,512]{1,0:T(8,128)(2,1)}, bf16[48,512]{1,0:T(8,128)(2,1)S(1)}, u32[]{:S(2)}, u32[]{:S(2)}) collective-permute-start(bf16[48,512]{1,0:T(8,128)(2,1)} %get-tuple-element.23), channel_id=1, source_target_pairs={{0,496},{1,497},{2,498},{3,499},{4,500},{5,501},{6,502},{7,503},{8... | collective-permute-start | bytes 147464 | tf_op jit(solution)/shard_map/ppermute | solution.py:269
  32.1 16.1 %all-to-all-start.1 = ((bf16[16,32,512]{2,1,0:T(8,128)(2,1)}), bf16[16,32,512]{2,1,0:T(8,128)(2,1)S(1)}, u32[]{:S(2)}, u32[]{:S(2)}) async-start(bf16[16,32,512]{2,1,0:T(8,128)(2,1)} %broadcast_in_dim.8), calls=%async_computation.1 | async-start | bytes 1048576 | tf_op jit(solution)/shard_map/all_to_all | solution.py:277
  39.6 10.5 %collective-permute-start.2 = (bf16[48,512]{1,0:T(8,128)(2,1)S(1)}, bf16[48,512]{1,0:T(8,128)(2,1)S(1)}, u32[]{:S(2)}, u32[]{:S(2)}) collective-permute-start(bf16[48,512]{1,0:T(8,128)(2,1)S(1)} %get-tuple-element.26), channel_id=1, source_target_pairs={{0,1},{1,0},{2,3},{3,2},{4,5},{5,4},{6,7},{7,6},{8,9},{9,8},{10,11... | collective-permute-start | bytes 147464 | tf_op jit(solution)/shard_map/ppermute | solution.py:274
  42.1 9.9 %collective-permute-start.3 = (bf16[48,512]{1,0:T(8,128)(2,1)S(1)}, bf16[48,512]{1,0:T(8,128)(2,1)S(1)}, u32[]{:S(2)}, u32[]{:S(2)}) collective-permute-start(bf16[48,512]{1,0:T(8,128)(2,1)S(1)} %get-tuple-element.25), channel_id=1, source_target_pairs={{0,15},{1,2},{2,1},{3,4},{4,3},{5,6},{6,5},{7,8},{8,7},{9,10},{10,... | collective-permute-start | bytes 147464 | tf_op jit(solution)/shard_map/ppermute | solution.py:275
  48.3 3.7 %copy-start.4 = (bf16[512,512]{1,0:T(8,128)(2,1)S(1)}, bf16[512,512]{1,0:T(8,128)(2,1)}, u32[]{:S(2)}) copy-start(bf16[512,512]{1,0:T(8,128)(2,1)} %w_sender_ref.1) | copy-start | bytes 1572868
  48.3 3.7 %copy-start.5 = (bf16[512,512]{1,0:T(8,128)(2,1)S(1)}, bf16[512,512]{1,0:T(8,128)(2,1)}, u32[]{:S(2)}) copy-start(bf16[512,512]{1,0:T(8,128)(2,1)} %w_message_ref.1) | copy-start | bytes 1572868
  48.3 3.7 %copy-start.6 = (bf16[512,512]{1,0:T(8,128)(2,1)S(1)}, bf16[512,512]{1,0:T(8,128)(2,1)}, u32[]{:S(2)}) copy-start(bf16[512,512]{1,0:T(8,128)(2,1)} %w_node_ref.1) | copy-start | bytes 1572868
  48.3 3.6 %copy-start.7 = (bf16[512,512]{1,0:T(8,128)(2,1)S(1)}, bf16[512,512]{1,0:T(8,128)(2,1)}, u32[]{:S(2)}) copy-start(bf16[512,512]{1,0:T(8,128)(2,1)} %w_gather_ref.1) | copy-start | bytes 1572868
  48.3 3.6 %copy-start.8 = (bf16[512,512]{1,0:T(8,128)(2,1)S(1)}, bf16[512,512]{1,0:T(8,128)(2,1)}, u32[]{:S(2)}) copy-start(bf16[512,512]{1,0:T(8,128)(2,1)} %w_node_out_ref.1) | copy-start | bytes 1572868
